TPU v7x, 256 devices: a whole 4x4x8 slice. The times are simulated.
256 devices in a mesh: section: 8 (over x, z_hi), dp: 16 (over z_lo, y), tensor: 2 (over core).
Axes of the slice: x: 4, y: 4, z: 8 (z_hi: 2, z_lo: 4; z = z_hi * 4 + z_lo), core: 2. Of those that a mesh axis runs over, the one named last changes fastest.
Arguments:
- section_inputs: bfloat16 [8, 4, 512, 8192], P('section', None, ('dp', 'tensor')), may hold values from -6 to 6
- top_grad: bfloat16 [4, 512, 8192], P(None, ('dp', 'tensor')), may hold values from -6 to 6
- value_weight: bfloat16 [8, 8192, 512], P('section', 'dp', 'tensor'), may hold values from -0.0625 to 0.0625
- output_weight: bfloat16 [8, 512, 8192], P('section', 'tensor', 'dp'), may hold values from -0.0625 to 0.0625
- owner_lengths: int32 [8, 2, 16], P('section', 'tensor'), may hold values from 196608 to 327680, as said below
- master_param: float32 [8, 2, 5242880], P('section', 'tensor', 'dp'), may hold values from -6 to 6
- moment1: float32 [8, 2, 5242880], P('section', 'tensor', 'dp'), may hold values from -4 to 4
- moment2: float32 [8, 2, 5242880], P('section', 'tensor', 'dp'), may hold values from 0.05 to 2
Outputs:
- input_grads: bfloat16 [8, 4, 512, 8192], P('section', None, ('dp', 'tensor'))
- new_param: float32 [8, 2, 5242880], P('section', 'tensor', 'dp')
- new_moment1: float32 [8, 2, 5242880], P('section', 'tensor', 'dp')
- new_moment2: float32 [8, 2, 5242880], P('section', 'tensor', 'dp')
Inputs may be any that keep to these rules, and one draw needn't show every extreme that they name: `owner_lengths`: every row of 16 lengths sums to 4194304; owner d's range starts at d * 262144 plus an offset of at most 32768 either way (owner 0 at 0), and some owner in every row has exactly 327680.
All inputs are finite; a program needn't handle non-finite values.
Results may differ from a plain program's by a relative error of at most 0.022.
Values may be sent and summed in bfloat16 or wider, within the bound.
A program may use at most 128 MiB of HBM per device.

v0:
```python
import math

import jax
import jax.numpy as jnp
from jax import lax
from jax.sharding import PartitionSpec as P

beta_one = 0.9
beta_two = 0.95
learn_rate = 0.001
decay_rate = 0.1
adam_eps = 1e-08
adam_step = 20.0


def shifted(block, axis, distance):
    devices = range(lax.axis_size(axis))
    route = [(i - distance, i) for i in devices if i - distance in devices]
    return lax.ppermute(block, axis, route)


def adam_update(master_value, first_moment, second_moment, grad_value):
    first_new = beta_one * first_moment + (1.0 - beta_one) * grad_value
    second_new = beta_two * second_moment + (1.0 - beta_two) * grad_value * grad_value
    corrected = (
        first_new
        / (1.0 - beta_one**adam_step)
        / (jnp.sqrt(second_new / (1.0 - beta_two**adam_step)) + adam_eps)
    )
    return (
        master_value - learn_rate * (corrected + decay_rate * master_value),
        first_new,
        second_new,
    )


def owner_slices(flat_grad, lengths, own_max):
    starts = jnp.cumsum(lengths, dtype=jnp.int32) - lengths
    extended = jnp.concatenate([flat_grad, jnp.zeros((own_max,), flat_grad.dtype)])
    offsets = jnp.arange(own_max, dtype=jnp.int32)

    def take_one(pair):
        begin, length = pair
        piece = lax.dynamic_slice_in_dim(extended, begin, own_max)
        return jnp.where(offsets < length, piece, jnp.zeros((), flat_grad.dtype))

    return lax.map(take_one, (starts, lengths))


def record(store, loop_item, slot_index, is_valid):
    return jnp.where(
        is_valid, lax.dynamic_update_index_in_dim(store, loop_item, slot_index, 0), store
    )


def local(
    section_inputs,
    top_grad,
    value_weight,
    output_weight,
    owner_lengths,
    master_param,
    moment1,
    moment2,
):
    sections = lax.axis_size("section")
    section_index = lax.axis_index("section")
    replicas = lax.axis_size("dp")
    micro_count = section_inputs.shape[1]
    half_rows = section_inputs.shape[2]
    model_width = section_inputs.shape[3]
    own_max = master_param.shape[-1]
    value_full, output_full = (
        lax.all_gather(value_weight[0], "dp", axis=0, tiled=True),
        lax.all_gather(output_weight[0], "dp", axis=1, tiled=True),
    )
    columns = value_full.shape[1]
    inputs_full = lax.all_gather(section_inputs[0], "tensor", axis=1, tiled=True)
    tokens = inputs_full.shape[1]
    grad_scale = 1.0 / math.sqrt(micro_count * tokens * replicas)
    at_top = section_index == sections - 1
    contract = (((1,), (1,)), ((), ()))
    rows_contract = (((0,), (0,)), ((), ()))
    source = lax.all_gather(top_grad, "tensor", axis=1, tiled=True)
    first_in = jnp.zeros((tokens, model_width), jnp.bfloat16)
    first_totals = (jnp.zeros((1, 1), jnp.float32), jnp.zeros((1, 1), jnp.float32))

    def step_body(step_index, loop_state):
        incoming, grad_store, vgrad_store, out_store, totals = loop_state
        micro_index = step_index - (sections - 1 - section_index)
        is_valid = jnp.logical_and(micro_index >= 0, micro_index < micro_count)
        slot_index = jnp.clip(micro_index, 0, micro_count - 1)
        arrived = jnp.where(
            at_top, lax.dynamic_index_in_dim(source, slot_index, 0, keepdims=False), incoming
        )
        value_grad = lax.dot_general(
            arrived, output_full, contract, preferred_element_type=jnp.float32
        ).astype(jnp.bfloat16)
        branch = lax.optimization_barrier(
            lax.dot_general(
                value_grad, value_full, contract, preferred_element_type=jnp.float32
            ).astype(jnp.bfloat16)
        ).astype(jnp.float32)
        summed = lax.psum(branch.astype(jnp.bfloat16), "tensor").astype(jnp.float32)
        full_rows = (arrived.astype(jnp.float32) + summed).astype(jnp.bfloat16)
        own_rows = lax.dynamic_slice_in_dim(
            full_rows, lax.axis_index("tensor") * half_rows, half_rows, 0
        )
        passed = shifted(full_rows, "section", -1)
        grad_store = record(grad_store, arrived, slot_index, is_valid)
        vgrad_store = record(vgrad_store, value_grad, slot_index, is_valid)
        out_store = record(out_store, own_rows, slot_index, is_valid)
        return (passed, grad_store, vgrad_store, out_store, totals)

    start_state = (
        first_in,
        jnp.zeros((micro_count, tokens, model_width), jnp.bfloat16),
        jnp.zeros((micro_count, tokens, columns), jnp.bfloat16),
        jnp.zeros((micro_count, half_rows, model_width), jnp.bfloat16),
        first_totals,
    )
    final_state = lax.fori_loop(0, sections + micro_count - 1, step_body, start_state)
    grad_store = final_state[1]
    vgrad_store = final_state[2]
    out_store = final_state[3]
    inputs_flat = inputs_full.reshape(-1, model_width)
    grads_flat = grad_store.reshape(-1, model_width)
    vgrad_flat = vgrad_store.reshape(-1, columns)
    values_flat = jnp.dot(inputs_flat, value_full, preferred_element_type=jnp.float32).astype(
        jnp.bfloat16
    )
    value_total = lax.dot_general(
        inputs_flat, vgrad_flat, rows_contract, preferred_element_type=jnp.float32
    )
    output_total = lax.dot_general(
        values_flat, grads_flat, rows_contract, preferred_element_type=jnp.float32
    )
    flat_grad = lax.optimization_barrier(
        jnp.concatenate(
            [
                (value_total * grad_scale).astype(jnp.bfloat16).reshape(-1),
                (output_total * grad_scale).astype(jnp.bfloat16).reshape(-1),
            ]
        )
    ).astype(jnp.float32)
    lengths = owner_lengths[0, 0]
    padded = owner_slices(flat_grad, lengths, own_max)
    reduced = lax.psum_scatter(
        padded.astype(jnp.bfloat16), "dp", scatter_dimension=0, tiled=True
    ).astype(jnp.float32)
    owned = reduced[0]
    updated = adam_update(master_param[0, 0], moment1[0, 0], moment2[0, 0], owned)
    return (out_store[None], updated[0][None, None], updated[1][None, None], updated[2][None, None])


def solution(mesh):
    in_specs = (
        P("section", None, ("dp", "tensor"), None),
        P(None, ("dp", "tensor"), None),
        P("section", "dp", "tensor"),
        P("section", "tensor", "dp"),
        P("section", "tensor", None),
        P("section", "tensor", "dp"),
        P("section", "tensor", "dp"),
        P("section", "tensor", "dp"),
    )
    out_specs = (
        P("section", None, ("dp", "tensor"), None),
        P("section", "tensor", "dp"),
        P("section", "tensor", "dp"),
        P("section", "tensor", "dp"),
    )
    return jax.shard_map(local, mesh=mesh, in_specs=in_specs, out_specs=out_specs, check_vma=False)
```

profile of v0, /device:TPU:97, one launch (start us, length us, event | category | flops | bytes accessed | tf_op | source)
XLA Modules:
  0.0 1804.1 jit_solution(4290262252221773403)
XLA Ops:
  10.2 17.9 all-gather.8.cloned.1.call-done
  28.1 19.0 %all-gather.14.cloned.1.call-done = bf16[1,4,32,8192]{3,2,1,0:T(8,128)(2,1)} async-done(((bf16[1,4,16,8192]{3,2,1,0:T(8,128)(2,1)}), bf16[1,4,32,8192]{3,2,1,0:T(8,128)(2,1)}) %all-gather.14.cloned.1.call-update) | async-done | bytes 2097168 | tf_op jit(solution)/shard_map/all_gather | solution.py:78
  47.1 76.7 %all-gather.12.cloned.1.call-done = bf16[1,8192,256]{2,1,0:T(8,128)(2,1)} async-done(((bf16[1,512,256]{2,1,0:T(8,128)(2,1)}), bf16[1,8192,256]{2,1,0:T(8,128)(2,1)}) %all-gather.12.cloned.1.call-update) | async-done | bytes 4194320 | tf_op jit(solution)/shard_map/all_gather | solution.py:74
  123.8 88.2 %all-gather.10.cloned.1.call-done = bf16[1,256,8192]{2,1,0:T(8,128)(2,1)} async-done(((bf16[1,256,512]{2,1,0:T(8,128)(2,1)}), bf16[1,256,8192]{2,1,0:T(8,128)(2,1)}) %all-gather.10.cloned.1.call-update) | async-done | bytes 4194320 | tf_op jit(solution)/shard_map/all_gather | solution.py:75
  213.3 784.0 %while.32 = (s32[]{:T(128)}, bf16[32,8192]{1,0:T(8,128)(2,1)S(1)}, bf16[4,32,8192]{2,1,0:T(8,128)(2,1)S(1)}, bf16[4,32,256]{2,1,0:T(8,128)(2,1)S(1)}, bf16[4,16,...) while((s32[]{:T(128)}, bf16[32,8192]{1,0:T(8,128)(2,1)S(1)}, ...), condition=%wide.region_2.3_spmd, body=%wide.region_0.2_spmd.sunk | while | flops 270680064 | bytes 36503956 | solution.py:122
  220.5 42.6 %all-reduce.7.cloned.1.call-done = bf16[32,8192]{1,0:T(8,128)(2,1)} async-done(((bf16[32,8192]{1,0:T(8,128)(2,1)}), bf16[32,8192]{1,0:T(8,128)(2,1)}) %all-reduce.7.cloned.1.call-update) | async-done | bytes 524304 | tf_op jit(solution)/shard_map/while/body/eval_jaxpr/psum | solution.py:104
  267.3 16.1 collective-permute-done
  290.6 44.0 %all-reduce.7.cloned.1.call-done = bf16[32,8192]{1,0:T(8,128)(2,1)} async-done(((bf16[32,8192]{1,0:T(8,128)(2,1)}), bf16[32,8192]{1,0:T(8,128)(2,1)}) %all-reduce.7.cloned.1.call-update) | async-done | bytes 524304 | tf_op jit(solution)/shard_map/while/body/eval_jaxpr/psum | solution.py:104
  338.7 16.1 collective-permute-done
  362.0 44.0 %all-reduce.7.cloned.1.call-done = bf16[32,8192]{1,0:T(8,128)(2,1)} async-done(((bf16[32,8192]{1,0:T(8,128)(2,1)}), bf16[32,8192]{1,0:T(8,128)(2,1)}) %all-reduce.7.cloned.1.call-update) | async-done | bytes 524304 | tf_op jit(solution)/shard_map/while/body/eval_jaxpr/psum | solution.py:104
  410.1 16.1 collective-permute-done
  433.4 43.9 %all-reduce.7.cloned.1.call-done = bf16[32,8192]{1,0:T(8,128)(2,1)} async-done(((bf16[32,8192]{1,0:T(8,128)(2,1)}), bf16[32,8192]{1,0:T(8,128)(2,1)}) %all-reduce.7.cloned.1.call-update) | async-done | bytes 524304 | tf_op jit(solution)/shard_map/while/body/eval_jaxpr/psum | solution.py:104
  481.5 16.1 collective-permute-done
  504.8 43.9 %all-reduce.7.cloned.1.call-done = bf16[32,8192]{1,0:T(8,128)(2,1)} async-done(((bf16[32,8192]{1,0:T(8,128)(2,1)}), bf16[32,8192]{1,0:T(8,128)(2,1)}) %all-reduce.7.cloned.1.call-update) | async-done | bytes 524304 | tf_op jit(solution)/shard_map/while/body/eval_jaxpr/psum | solution.py:104
  552.9 16.1 collective-permute-done
  576.1 43.9 %all-reduce.7.cloned.1.call-done = bf16[32,8192]{1,0:T(8,128)(2,1)} async-done(((bf16[32,8192]{1,0:T(8,128)(2,1)}), bf16[32,8192]{1,0:T(8,128)(2,1)}) %all-reduce.7.cloned.1.call-update) | async-done | bytes 524304 | tf_op jit(solution)/shard_map/while/body/eval_jaxpr/psum | solution.py:104
  624.3 16.1 collective-permute-done
  647.5 43.9 %all-reduce.7.cloned.1.call-done = bf16[32,8192]{1,0:T(8,128)(2,1)} async-done(((bf16[32,8192]{1,0:T(8,128)(2,1)}), bf16[32,8192]{1,0:T(8,128)(2,1)}) %all-reduce.7.cloned.1.call-update) | async-done | bytes 524304 | tf_op jit(solution)/shard_map/while/body/eval_jaxpr/psum | solution.py:104
  695.7 16.1 collective-permute-done
  718.9 43.9 %all-reduce.7.cloned.1.call-done = bf16[32,8192]{1,0:T(8,128)(2,1)} async-done(((bf16[32,8192]{1,0:T(8,128)(2,1)}), bf16[32,8192]{1,0:T(8,128)(2,1)}) %all-reduce.7.cloned.1.call-update) | async-done | bytes 524304 | tf_op jit(solution)/shard_map/while/body/eval_jaxpr/psum | solution.py:104
  767.0 16.1 collective-permute-done
  790.3 43.9 %all-reduce.7.cloned.1.call-done = bf16[32,8192]{1,0:T(8,128)(2,1)} async-done(((bf16[32,8192]{1,0:T(8,128)(2,1)}), bf16[32,8192]{1,0:T(8,128)(2,1)}) %all-reduce.7.cloned.1.call-update) | async-done | bytes 524304 | tf_op jit(solution)/shard_map/while/body/eval_jaxpr/psum | solution.py:104
  838.4 16.1 collective-permute-done
  861.7 43.9 %all-reduce.7.cloned.1.call-done = bf16[32,8192]{1,0:T(8,128)(2,1)} async-done(((bf16[32,8192]{1,0:T(8,128)(2,1)}), bf16[32,8192]{1,0:T(8,128)(2,1)}) %all-reduce.7.cloned.1.call-update) | async-done | bytes 524304 | tf_op jit(solution)/shard_map/while/body/eval_jaxpr/psum | solution.py:104
  909.8 16.1 collective-permute-done
  933.1 43.9 %all-reduce.7.cloned.1.call-done = bf16[32,8192]{1,0:T(8,128)(2,1)} async-done(((bf16[32,8192]{1,0:T(8,128)(2,1)}), bf16[32,8192]{1,0:T(8,128)(2,1)}) %all-reduce.7.cloned.1.call-update) | async-done | bytes 524304 | tf_op jit(solution)/shard_map/while/body/eval_jaxpr/psum | solution.py:104
  981.2 16.1 collective-permute-done
  1028.9 17.9 pad_maximum_fusion
  1046.8 9.3 pad_convert_fusion
  1056.1 473.3 %while.33 = (s32[]{:T(128)}, bf16[16,327680]{1,0:T(8,128)(2,1)}, s32[16]{0:T(128)S(1)}, s32[16]{0:T(128)S(1)}, f32[4521984]{0:T(1024)}, /*index=5*/s32[]{:T(128)}, s32[]{:T(128)}, s32[]{:T(128)}) while((s32[]{:T(128)}, bf16[16,327680]{1,0:T(8,128)(2,1)}, s32[16]{0:T(128)S(1)}, s32[16]{0:T(128)S(1)}, f32[4521984]{0:T(1024)}, ...), condition=%wide.region_5.6_spmd.clone, body=%wide.region_4.5_spmd.clone.sunk | while | flops 655365 | bytes 5243035 | solution.py:47
  1061.6 24.1 %dynamic_update_slice.18 = bf16[16,327680]{1,0:T(8,128)(2,1)} dynamic-update-slice(bf16[16,327680]{1,0:T(8,128)(2,1)} %get-tuple-element.484, f32[1,327680]{1,0:T(1,128)S(1)} %bitcast.88, s32[]{:T(128)} %get-tuple-element.483, s32[]{:T(128)} %constant.131.clone.1..sunk.1) | dynamic-update-slice | bytes 2621444 | tf_op jit(solution)/shard_map/while/body/jit(dynamic_update_index_in_dim)/dynamic_update_slice | solution.py:47
  1091.2 24.1 %dynamic_update_slice.18 = bf16[16,327680]{1,0:T(8,128)(2,1)} dynamic-update-slice(bf16[16,327680]{1,0:T(8,128)(2,1)} %get-tuple-element.484, f32[1,327680]{1,0:T(1,128)S(1)} %bitcast.88, s32[]{:T(128)} %get-tuple-element.483, s32[]{:T(128)} %constant.131.clone.1..sunk.1) | dynamic-update-slice | bytes 2621444 | tf_op jit(solution)/shard_map/while/body/jit(dynamic_update_index_in_dim)/dynamic_update_slice | solution.py:47
  1120.7 24.1 %dynamic_update_slice.18 = bf16[16,327680]{1,0:T(8,128)(2,1)} dynamic-update-slice(bf16[16,327680]{1,0:T(8,128)(2,1)} %get-tuple-element.484, f32[1,327680]{1,0:T(1,128)S(1)} %bitcast.88, s32[]{:T(128)} %get-tuple-element.483, s32[]{:T(128)} %constant.131.clone.1..sunk.1) | dynamic-update-slice | bytes 2621444 | tf_op jit(solution)/shard_map/while/body/jit(dynamic_update_index_in_dim)/dynamic_update_slice | solution.py:47
  1150.3 24.1 %dynamic_update_slice.18 = bf16[16,327680]{1,0:T(8,128)(2,1)} dynamic-update-slice(bf16[16,327680]{1,0:T(8,128)(2,1)} %get-tuple-element.484, f32[1,327680]{1,0:T(1,128)S(1)} %bitcast.88, s32[]{:T(128)} %get-tuple-element.483, s32[]{:T(128)} %constant.131.clone.1..sunk.1) | dynamic-update-slice | bytes 2621444 | tf_op jit(solution)/shard_map/while/body/jit(dynamic_update_index_in_dim)/dynamic_update_slice | solution.py:47
  1179.9 24.1 %dynamic_update_slice.18 = bf16[16,327680]{1,0:T(8,128)(2,1)} dynamic-update-slice(bf16[16,327680]{1,0:T(8,128)(2,1)} %get-tuple-element.484, f32[1,327680]{1,0:T(1,128)S(1)} %bitcast.88, s32[]{:T(128)} %get-tuple-element.483, s32[]{:T(128)} %constant.131.clone.1..sunk.1) | dynamic-update-slice | bytes 2621444 | tf_op jit(solution)/shard_map/while/body/jit(dynamic_update_index_in_dim)/dynamic_update_slice | solution.py:47
  1209.4 24.1 %dynamic_update_slice.18 = bf16[16,327680]{1,0:T(8,128)(2,1)} dynamic-update-slice(bf16[16,327680]{1,0:T(8,128)(2,1)} %get-tuple-element.484, f32[1,327680]{1,0:T(1,128)S(1)} %bitcast.88, s32[]{:T(128)} %get-tuple-element.483, s32[]{:T(128)} %constant.131.clone.1..sunk.1) | dynamic-update-slice | bytes 2621444 | tf_op jit(solution)/shard_map/while/body/jit(dynamic_update_index_in_dim)/dynamic_update_slice | solution.py:47
  1239.0 24.1 %dynamic_update_slice.18 = bf16[16,327680]{1,0:T(8,128)(2,1)} dynamic-update-slice(bf16[16,327680]{1,0:T(8,128)(2,1)} %get-tuple-element.484, f32[1,327680]{1,0:T(1,128)S(1)} %bitcast.88, s32[]{:T(128)} %get-tuple-element.483, s32[]{:T(128)} %constant.131.clone.1..sunk.1) | dynamic-update-slice | bytes 2621444 | tf_op jit(solution)/shard_map/while/body/jit(dynamic_update_index_in_dim)/dynamic_update_slice | solution.py:47
  1268.5 24.1 %dynamic_update_slice.18 = bf16[16,327680]{1,0:T(8,128)(2,1)} dynamic-update-slice(bf16[16,327680]{1,0:T(8,128)(2,1)} %get-tuple-element.484, f32[1,327680]{1,0:T(1,128)S(1)} %bitcast.88, s32[]{:T(128)} %get-tuple-element.483, s32[]{:T(128)} %constant.131.clone.1..sunk.1) | dynamic-update-slice | bytes 2621444 | tf_op jit(solution)/shard_map/while/body/jit(dynamic_update_index_in_dim)/dynamic_update_slice | solution.py:47
  1298.1 24.1 %dynamic_update_slice.18 = bf16[16,327680]{1,0:T(8,128)(2,1)} dynamic-update-slice(bf16[16,327680]{1,0:T(8,128)(2,1)} %get-tuple-element.484, f32[1,327680]{1,0:T(1,128)S(1)} %bitcast.88, s32[]{:T(128)} %get-tuple-element.483, s32[]{:T(128)} %constant.131.clone.1..sunk.1) | dynamic-update-slice | bytes 2621444 | tf_op jit(solution)/shard_map/while/body/jit(dynamic_update_index_in_dim)/dynamic_update_slice | solution.py:47
  1327.7 24.1 %dynamic_update_slice.18 = bf16[16,327680]{1,0:T(8,128)(2,1)} dynamic-update-slice(bf16[16,327680]{1,0:T(8,128)(2,1)} %get-tuple-element.484, f32[1,327680]{1,0:T(1,128)S(1)} %bitcast.88, s32[]{:T(128)} %get-tuple-element.483, s32[]{:T(128)} %constant.131.clone.1..sunk.1) | dynamic-update-slice | bytes 2621444 | tf_op jit(solution)/shard_map/while/body/jit(dynamic_update_index_in_dim)/dynamic_update_slice | solution.py:47
  1357.3 24.1 %dynamic_update_slice.18 = bf16[16,327680]{1,0:T(8,128)(2,1)} dynamic-update-slice(bf16[16,327680]{1,0:T(8,128)(2,1)} %get-tuple-element.484, f32[1,327680]{1,0:T(1,128)S(1)} %bitcast.88, s32[]{:T(128)} %get-tuple-element.483, s32[]{:T(128)} %constant.131.clone.1..sunk.1) | dynamic-update-slice | bytes 2621444 | tf_op jit(solution)/shard_map/while/body/jit(dynamic_update_index_in_dim)/dynamic_update_slice | solution.py:47
  1386.9 24.1 %dynamic_update_slice.18 = bf16[16,327680]{1,0:T(8,128)(2,1)} dynamic-update-slice(bf16[16,327680]{1,0:T(8,128)(2,1)} %get-tuple-element.484, f32[1,327680]{1,0:T(1,128)S(1)} %bitcast.88, s32[]{:T(128)} %get-tuple-element.483, s32[]{:T(128)} %constant.131.clone.1..sunk.1) | dynamic-update-slice | bytes 2621444 | tf_op jit(solution)/shard_map/while/body/jit(dynamic_update_index_in_dim)/dynamic_update_slice | solution.py:47
  1416.5 24.1 %dynamic_update_slice.18 = bf16[16,327680]{1,0:T(8,128)(2,1)} dynamic-update-slice(bf16[16,327680]{1,0:T(8,128)(2,1)} %get-tuple-element.484, f32[1,327680]{1,0:T(1,128)S(1)} %bitcast.88, s32[]{:T(128)} %get-tuple-element.483, s32[]{:T(128)} %constant.131.clone.1..sunk.1) | dynamic-update-slice | bytes 2621444 | tf_op jit(solution)/shard_map/while/body/jit(dynamic_update_index_in_dim)/dynamic_update_slice | solution.py:47
  1446.1 24.1 %dynamic_update_slice.18 = bf16[16,327680]{1,0:T(8,128)(2,1)} dynamic-update-slice(bf16[16,327680]{1,0:T(8,128)(2,1)} %get-tuple-element.484, f32[1,327680]{1,0:T(1,128)S(1)} %bitcast.88, s32[]{:T(128)} %get-tuple-element.483, s32[]{:T(128)} %constant.131.clone.1..sunk.1) | dynamic-update-slice | bytes 2621444 | tf_op jit(solution)/shard_map/while/body/jit(dynamic_update_index_in_dim)/dynamic_update_slice | solution.py:47
  1475.7 24.1 %dynamic_update_slice.18 = bf16[16,327680]{1,0:T(8,128)(2,1)} dynamic-update-slice(bf16[16,327680]{1,0:T(8,128)(2,1)} %get-tuple-element.484, f32[1,327680]{1,0:T(1,128)S(1)} %bitcast.88, s32[]{:T(128)} %get-tuple-element.483, s32[]{:T(128)} %constant.131.clone.1..sunk.1) | dynamic-update-slice | bytes 2621444 | tf_op jit(solution)/shard_map/while/body/jit(dynamic_update_index_in_dim)/dynamic_update_slice | solution.py:47
  1505.3 24.1 %dynamic_update_slice.18 = bf16[16,327680]{1,0:T(8,128)(2,1)} dynamic-update-slice(bf16[16,327680]{1,0:T(8,128)(2,1)} %get-tuple-element.484, f32[1,327680]{1,0:T(1,128)S(1)} %bitcast.88, s32[]{:T(128)} %get-tuple-element.483, s32[]{:T(128)} %constant.131.clone.1..sunk.1) | dynamic-update-slice | bytes 2621444 | tf_op jit(solution)/shard_map/while/body/jit(dynamic_update_index_in_dim)/dynamic_update_slice | solution.py:47
  1530.6 254.6 %all-reduce.5.cloned.1.call-done = bf16[16,327680]{1,0:T(8,128)(2,1)} async-done(((bf16[16,327680]{1,0:T(8,128)(2,1)}), bf16[16,327680]{1,0:T(8,128)(2,1)}) %all-reduce.5.cloned.1.call-update) | async-done | bytes 10485776
  1785.2 12.4 multiply_subtract_fusion
  (195 shorter events, 218.3 us)
Async XLA Ops:
  7.2 2.8 copy-start.5
  7.2 20.9 %all-gather.8.cloned.1.call-start = ((), (), s32[]{:S(2)}) async-start(), calls=%async_computation | async-start | bytes 3145728 | tf_op jit(solution)/shard_map/all_gather | solution.py:84
  7.9 39.2 %all-gather.14.cloned.1.call-start = ((), (), s32[]{:S(2)}) async-start(), calls=%async_computation.3 | async-start | bytes 3145728 | tf_op jit(solution)/shard_map/all_gather | solution.py:78
  8.7 115.1 %all-gather.12.cloned.1.call-start = ((), (), s32[]{:S(2)}) async-start(), calls=%async_computation.2 | async-start | bytes 4456448 | tf_op jit(solution)/shard_map/all_gather | solution.py:74
  9.4 202.6 %all-gather.10.cloned.1.call-start = ((), (), s32[]{:S(2)}) async-start(), calls=%async_computation.1 | async-start | bytes 4456448 | tf_op jit(solution)/shard_map/all_gather | solution.py:75
  213.3 49.8 %all-reduce.7.cloned.1.call-start = ((), (), s32[]{:S(2)}) async-start(), calls=%async_computation.5 | async-start | bytes 1048576 | tf_op jit(solution)/shard_map/while/body/eval_jaxpr/psum | solution.py:104
  214.7 3.7 copy-start
  264.3 19.1 %collective-permute-start = (bf16[32,8192]{1,0:T(8,128)(2,1)S(1)}, bf16[32,8192]{1,0:T(8,128)(2,1)S(1)}, u32[]{:S(2)}, u32[]{:S(2)}) collective-permute-start(bf16[32,8192]{1,0:T(8,128)(2,1)S(1)} %add_convert_fusion.2), channel_id=1, source_target_pairs={{32,0},{64,32},{96,64},{128,96},{160,128},{192,160},{224,192},{33,... | collective-permute-start | bytes 1572872 | tf_op jit(solution)/shard_map/while/body/eval_jaxpr/ppermute | solution.py:19
  283.4 51.1 %all-reduce.7.cloned.1.call-start = ((), (), s32[]{:S(2)}) async-start(), calls=%async_computation.5 | async-start | bytes 1048576 | tf_op jit(solution)/shard_map/while/body/eval_jaxpr/psum | solution.py:104
  284.7 3.7 copy-start
  335.7 19.1 %collective-permute-start = (bf16[32,8192]{1,0:T(8,128)(2,1)S(1)}, bf16[32,8192]{1,0:T(8,128)(2,1)S(1)}, u32[]{:S(2)}, u32[]{:S(2)}) collective-permute-start(bf16[32,8192]{1,0:T(8,128)(2,1)S(1)} %add_convert_fusion.2), channel_id=1, source_target_pairs={{32,0},{64,32},{96,64},{128,96},{160,128},{192,160},{224,192},{33,... | collective-permute-start | bytes 1572872 | tf_op jit(solution)/shard_map/while/body/eval_jaxpr/ppermute | solution.py:19
  354.8 51.1 %all-reduce.7.cloned.1.call-start = ((), (), s32[]{:S(2)}) async-start(), calls=%async_computation.5 | async-start | bytes 1048576 | tf_op jit(solution)/shard_map/while/body/eval_jaxpr/psum | solution.py:104
  356.1 3.7 copy-start
  407.1 19.1 %collective-permute-start = (bf16[32,8192]{1,0:T(8,128)(2,1)S(1)}, bf16[32,8192]{1,0:T(8,128)(2,1)S(1)}, u32[]{:S(2)}, u32[]{:S(2)}) collective-permute-start(bf16[32,8192]{1,0:T(8,128)(2,1)S(1)} %add_convert_fusion.2), channel_id=1, source_target_pairs={{32,0},{64,32},{96,64},{128,96},{160,128},{192,160},{224,192},{33,... | collective-permute-start | bytes 1572872 | tf_op jit(solution)/shard_map/while/body/eval_jaxpr/ppermute | solution.py:19
  426.2 51.1 %all-reduce.7.cloned.1.call-start = ((), (), s32[]{:S(2)}) async-start(), calls=%async_computation.5 | async-start | bytes 1048576 | tf_op jit(solution)/shard_map/while/body/eval_jaxpr/psum | solution.py:104
  427.5 3.7 copy-start
  478.5 19.1 %collective-permute-start = (bf16[32,8192]{1,0:T(8,128)(2,1)S(1)}, bf16[32,8192]{1,0:T(8,128)(2,1)S(1)}, u32[]{:S(2)}, u32[]{:S(2)}) collective-permute-start(bf16[32,8192]{1,0:T(8,128)(2,1)S(1)} %add_convert_fusion.2), channel_id=1, source_target_pairs={{32,0},{64,32},{96,64},{128,96},{160,128},{192,160},{224,192},{33,... | collective-permute-start | bytes 1572872 | tf_op jit(solution)/shard_map/while/body/eval_jaxpr/ppermute | solution.py:19
  497.6 51.1 %all-reduce.7.cloned.1.call-start = ((), (), s32[]{:S(2)}) async-start(), calls=%async_computation.5 | async-start | bytes 1048576 | tf_op jit(solution)/shard_map/while/body/eval_jaxpr/psum | solution.py:104
  498.9 3.7 copy-start
  549.9 19.1 %collective-permute-start = (bf16[32,8192]{1,0:T(8,128)(2,1)S(1)}, bf16[32,8192]{1,0:T(8,128)(2,1)S(1)}, u32[]{:S(2)}, u32[]{:S(2)}) collective-permute-start(bf16[32,8192]{1,0:T(8,128)(2,1)S(1)} %add_convert_fusion.2), channel_id=1, source_target_pairs={{32,0},{64,32},{96,64},{128,96},{160,128},{192,160},{224,192},{33,... | collective-permute-start | bytes 1572872 | tf_op jit(solution)/shard_map/while/body/eval_jaxpr/ppermute | solution.py:19
  569.0 51.1 %all-reduce.7.cloned.1.call-start = ((), (), s32[]{:S(2)}) async-start(), calls=%async_computation.5 | async-start | bytes 1048576 | tf_op jit(solution)/shard_map/while/body/eval_jaxpr/psum | solution.py:104
  570.3 3.7 copy-start
  621.3 19.1 %collective-permute-start = (bf16[32,8192]{1,0:T(8,128)(2,1)S(1)}, bf16[32,8192]{1,0:T(8,128)(2,1)S(1)}, u32[]{:S(2)}, u32[]{:S(2)}) collective-permute-start(bf16[32,8192]{1,0:T(8,128)(2,1)S(1)} %add_convert_fusion.2), channel_id=1, source_target_pairs={{32,0},{64,32},{96,64},{128,96},{160,128},{192,160},{224,192},{33,... | collective-permute-start | bytes 1572872 | tf_op jit(solution)/shard_map/while/body/eval_jaxpr/ppermute | solution.py:19
  640.4 51.1 %all-reduce.7.cloned.1.call-start = ((), (), s32[]{:S(2)}) async-start(), calls=%async_computation.5 | async-start | bytes 1048576 | tf_op jit(solution)/shard_map/while/body/eval_jaxpr/psum | solution.py:104
  641.6 3.7 copy-start
  692.6 19.1 %collective-permute-start = (bf16[32,8192]{1,0:T(8,128)(2,1)S(1)}, bf16[32,8192]{1,0:T(8,128)(2,1)S(1)}, u32[]{:S(2)}, u32[]{:S(2)}) collective-permute-start(bf16[32,8192]{1,0:T(8,128)(2,1)S(1)} %add_convert_fusion.2), channel_id=1, source_target_pairs={{32,0},{64,32},{96,64},{128,96},{160,128},{192,160},{224,192},{33,... | collective-permute-start | bytes 1572872 | tf_op jit(solution)/shard_map/while/body/eval_jaxpr/ppermute | solution.py:19
  711.7 51.1 %all-reduce.7.cloned.1.call-start = ((), (), s32[]{:S(2)}) async-start(), calls=%async_computation.5 | async-start | bytes 1048576 | tf_op jit(solution)/shard_map/while/body/eval_jaxpr/psum | solution.py:104
  713.0 3.7 copy-start
  764.0 19.1 %collective-permute-start = (bf16[32,8192]{1,0:T(8,128)(2,1)S(1)}, bf16[32,8192]{1,0:T(8,128)(2,1)S(1)}, u32[]{:S(2)}, u32[]{:S(2)}) collective-permute-start(bf16[32,8192]{1,0:T(8,128)(2,1)S(1)} %add_convert_fusion.2), channel_id=1, source_target_pairs={{32,0},{64,32},{96,64},{128,96},{160,128},{192,160},{224,192},{33,... | collective-permute-start | bytes 1572872 | tf_op jit(solution)/shard_map/while/body/eval_jaxpr/ppermute | solution.py:19
  783.1 51.1 %all-reduce.7.cloned.1.call-start = ((), (), s32[]{:S(2)}) async-start(), calls=%async_computation.5 | async-start | bytes 1048576 | tf_op jit(solution)/shard_map/while/body/eval_jaxpr/psum | solution.py:104
  784.4 3.7 copy-start
  835.4 19.1 %collective-permute-start = (bf16[32,8192]{1,0:T(8,128)(2,1)S(1)}, bf16[32,8192]{1,0:T(8,128)(2,1)S(1)}, u32[]{:S(2)}, u32[]{:S(2)}) collective-permute-start(bf16[32,8192]{1,0:T(8,128)(2,1)S(1)} %add_convert_fusion.2), channel_id=1, source_target_pairs={{32,0},{64,32},{96,64},{128,96},{160,128},{192,160},{224,192},{33,... | collective-permute-start | bytes 1572872 | tf_op jit(solution)/shard_map/while/body/eval_jaxpr/ppermute | solution.py:19
  854.5 51.1 %all-reduce.7.cloned.1.call-start = ((), (), s32[]{:S(2)}) async-start(), calls=%async_computation.5 | async-start | bytes 1048576 | tf_op jit(solution)/shard_map/while/body/eval_jaxpr/psum | solution.py:104
  855.8 3.7 copy-start
  906.8 19.1 %collective-permute-start = (bf16[32,8192]{1,0:T(8,128)(2,1)S(1)}, bf16[32,8192]{1,0:T(8,128)(2,1)S(1)}, u32[]{:S(2)}, u32[]{:S(2)}) collective-permute-start(bf16[32,8192]{1,0:T(8,128)(2,1)S(1)} %add_convert_fusion.2), channel_id=1, source_target_pairs={{32,0},{64,32},{96,64},{128,96},{160,128},{192,160},{224,192},{33,... | collective-permute-start | bytes 1572872 | tf_op jit(solution)/shard_map/while/body/eval_jaxpr/ppermute | solution.py:19
  925.9 51.1 %all-reduce.7.cloned.1.call-start = ((), (), s32[]{:S(2)}) async-start(), calls=%async_computation.5 | async-start | bytes 1048576 | tf_op jit(solution)/shard_map/while/body/eval_jaxpr/psum | solution.py:104
  927.2 3.7 copy-start
  978.2 19.1 %collective-permute-start = (bf16[32,8192]{1,0:T(8,128)(2,1)S(1)}, bf16[32,8192]{1,0:T(8,128)(2,1)S(1)}, u32[]{:S(2)}, u32[]{:S(2)}) collective-permute-start(bf16[32,8192]{1,0:T(8,128)(2,1)S(1)} %add_convert_fusion.2), channel_id=1, source_target_pairs={{32,0},{64,32},{96,64},{128,96},{160,128},{192,160},{224,192},{33,... | collective-permute-start | bytes 1572872 | tf_op jit(solution)/shard_map/while/body/eval_jaxpr/ppermute | solution.py:19
  997.3 787.9 %all-reduce.5.cloned.1.call-start = ((), (), s32[]{:S(2)}) async-start(), calls=%async_computation.4 | async-start | bytes 20971520
  1005.1 5.5 copy-start.2
  1020.3 8.6 copy-start.1
  1529.4 0.7 copy-start.6
  1529.4 255.9 %copy-start.3 = (f32[1,1,327680]{2,1,0:T(1,128)S(1)}, f32[1,1,327680]{2,1,0:T(1,128)}, u32[]{:S(2)}) copy-start(f32[1,1,327680]{2,1,0:T(1,128)} %param.17) | copy-start | bytes 3932164
  1529.4 255.9 %copy-start.4 = (f32[1,1,327680]{2,1,0:T(1,128)S(1)}, f32[1,1,327680]{2,1,0:T(1,128)}, u32[]{:S(2)}) copy-start(f32[1,1,327680]{2,1,0:T(1,128)} %param.18) | copy-start | bytes 3932164
Sparse Core Ops, SparseCore 0:
  9.8 18.2 all-gather.7
  29.9 17.1 all-gather.13
  48.9 74.8 all-gather.11
  125.5 86.5 all-gather.9
  220.7 42.4 all-reduce.6
  290.7 43.7 all-reduce.6
  362.1 43.7 all-reduce.6
  433.5 43.7 all-reduce.6
  504.9 43.7 all-reduce.6
  576.3 43.7 all-reduce.6
  647.6 43.7 all-reduce.6
  719.0 43.7 all-reduce.6
  790.4 43.7 all-reduce.6
  861.8 43.7 all-reduce.6
  933.2 43.7 all-reduce.6
  1529.5 255.6 all-reduce.4
where the time goes:
time: 1820 us; the launch traced here: 1800 us
  waiting for transfers between devices  1120 us (62%)
  local copies, waits for them, and re-layouts  427 us (23%)
  other arithmetic  123 us (7%)
  matrix products  75.2 us (4%)
  loops' own time  31.8 us (2%)
    psum x11, waiting for transfers between devices, step_body(): summed = lax.psum(branch.astype(jnp.bfloat16), 'tensor').astype(jnp.float32)  482 us
    dynamic_update_slice x16, local copies, waits for them, and re-layouts, owner_slices(): return lax.map(take_one, (starts, lengths))  385 us
    unnamed x6, waiting for transfers between devices  257 us
    ppermute x11, waiting for transfers between devices, shifted(): return lax.ppermute(block, axis, route)  177 us
    all_gather x1, waiting for transfers between devices, local(): lax.all_gather(output_weight[0], 'dp', axis=1, tiled=True)  88.2 us
    all_gather x1, waiting for transfers between devices, local(): lax.all_gather(value_weight[0], 'dp', axis=0, tiled=True)  76.7 us
    dot_general x11, matrix products, step_body(): lax.dot_general(arrived, output_full, contract, preferred_element_type=jn...  40.6 us
    select_n x16, other arithmetic, take_one(): return jnp.where(offsets < length, piece, jnp.zeros((), flat_grad.dtype))  38 us
  transfers between devices with their start and end apart: 27, of which 27 were waited for; matrix products, arithmetic and copies ran while one was open for 1% of the time, Pallas kernels for 0%

commit v1 on v0

v1 whole, which is shorter than its diff:
```python
import functools
import math

import jax
import jax.numpy as jnp
from jax import lax
from jax.experimental import pallas as pl
from jax.experimental.pallas import tpu as pltpu
from jax.sharding import PartitionSpec as P

MESH = pl.DeviceIdType.MESH
BF16 = jnp.bfloat16
F32 = jnp.float32

beta_one = 0.9
beta_two = 0.95
learn_rate = 0.001
decay_rate = 0.1
adam_eps = 1e-08
adam_step = 20.0

CHUNKS = 8
NT = (((1,), (1,)), ((), ()))
NN = (((1,), (0,)), ((), ()))
TN = (((0,), (0,)), ((), ()))


def dot(a, b, dims):
    return lax.dot_general(a, b, dims, preferred_element_type=F32)


def device(x, y, z, t):
    return (2 * x + lax.div(z, 4), lax.rem(z, 4) * 4 + y, t)


def aligned(start, size):
    return pl.ds(pl.multiple_of(start, size), size)


def wait_bytes(ref, sem):
    pltpu.make_async_copy(ref, ref, sem).wait()


def relay_kernel(
    xin, top, vw, ow,
    out, vwin, owin,
    gin, gout, xrow, vst, ost, vd, od, pbuf, rsb, vg, gd, pv, rsv, val, xd, accv, acco, dvb, dob,
    s_x, s_w1, s_w2, s_top, s_rs, s_ag, s_hop, s_out, s_gd, s_vg, s_rsv, s_agv, s_val, s_xd, s_own,
    r_x, r_w1, r_w2, r_g, r_rs, r_ag, r_gd, r_vg, r_rsv, r_agv, r_val, r_xd, r_own, r_out,
):
    sec = lax.axis_index("section")
    dp = lax.axis_index("dp")
    t = lax.axis_index("tensor")
    x = lax.div(sec, 2)
    zl = lax.div(dp, 4)
    y = lax.rem(dp, 4)
    z = lax.rem(sec, 2) * 4 + zl

    def is_me(to):
        return jnp.logical_and(jnp.logical_and(to[0] == sec, to[1] == dp), to[2] == t)

    def send(src, dst, ssem, rsem, to):
        mine = is_me(to)

        @pl.when(mine)
        def _():
            pltpu.make_async_copy(src, dst, rsem).start()

        @pl.when(jnp.logical_not(mine))
        def _():
            pltpu.make_async_remote_copy(src, dst, ssem, rsem, device_id=to, device_id_type=MESH).start()

    def sent(src, ssem, to):
        @pl.when(jnp.logical_not(is_me(to)))
        def _():
            wait_bytes(src, ssem)

    def push(src, dst, ssem, rsem, to):
        pltpu.make_async_remote_copy(src, dst, ssem, rsem, device_id=to, device_id_type=MESH).start()

    w1_to = device(zl, y, sec, t)
    send(vw, vst, s_w1.at[0], r_w1.at[0], w1_to)
    send(ow, ost, s_w1.at[1], r_w1.at[1], w1_to)

    half = lax.div(zl, 2)
    row16 = aligned(lax.rem(zl, 2) * 32 + t * 16, 16)
    top_sender = jnp.logical_or(z < 2, z >= 6)

    def top_parts():
        for mb in range(4):
            for t2 in range(2):
                src = top.at[mb, :, aligned(x * 2048 + t2 * 1024, 1024)]
                yield mb * 2 + t2, src, mb * 2 + half, device(x, y, 7, t2)

    @pl.when(top_sender)
    def _():
        for k, src, c, to in top_parts():
            send(src, gin.at[c, row16, :], s_top.at[k], r_g.at[c], to)

    def x_parts():
        for x2 in range(4):
            for t2 in range(2):
                src = xin.at[:, :, pl.ds(x2 * 2048 + t2 * 1024, 1024)]
                yield x2 * 2 + t2, src, device(x2, y, sec, t2)

    for k, src, to in x_parts():
        send(src, xrow.at[:, half, row16, :], s_x.at[k], r_x, to)

    wait_bytes(vst, r_w1.at[0])
    wait_bytes(ost, r_w1.at[1])

    def w2_parts():
        rows = aligned(lax.rem(y, 2) * 512, 512)
        cols = aligned(t * 256, 256)
        for y2 in range(4):
            to = device(x, y2, z, lax.div(y, 2))
            yield y2, vst, vd.at[rows, cols], 0, to
            yield 4 + y2, ost, od.at[cols, rows], 1, to

    for k, src, dst, r, to in w2_parts():
        send(src, dst, s_w2.at[k], r_w2.at[r], to)
    wait_bytes(vd, r_w2.at[0])
    wait_bytes(od, r_w2.at[1])

    def peers():
        for k in range(1, 8):
            yield k - 1, lax.rem(x + k // 2, 4), lax.rem(t + k % 2, 2)

    def y_peers():
        for k in range(1, 4):
            yield k - 1, lax.rem(y + k, 4)

    def xd_parts():
        for y2 in range(4):
            yield y2, xrow.at[:, :, :, pl.ds(y2 * 256, 256)], device(x, y2, z, t)

    def values_stage():
        wait_bytes(xrow, r_x)
        for k, src, to in xd_parts():
            send(src, xd.at[y], s_xd.at[k], r_xd, to)

        def block(i, carry):
            rows = xrow[lax.div(i, 2), lax.rem(i, 2)]
            pv[aligned(i * 64, 64), :] = dot(rows, vd[...], NN).astype(BF16)
            return carry

        lax.fori_loop(0, 8, block, 0)
        for k, x2, t2 in peers():
            push(
                pv.at[aligned(x2 * 128, 128), aligned(t2 * 256, 256)], rsv.at[k], s_rsv, r_rsv, device(x2, y, z, t2)
            )
        wait_bytes(rsv, r_rsv)
        rows, cols = aligned(x * 128, 128), aligned(t * 256, 256)
        total = pv[rows, cols].astype(F32)
        for k in range(7):
            total = total + rsv[k].astype(F32)
        val[y, rows, cols] = total.astype(BF16)
        mine = val.at[y, rows, cols]
        for k, x2, t2 in peers():
            push(mine, mine, s_agv, r_agv, device(x2, y, z, t2))
        wait_bytes(rsv, r_agv)
        for k, y2 in y_peers():
            push(val.at[y], val.at[y], s_val.at[k], r_val, device(x, y2, z, t))

    @pl.when(z < 4)
    def _():
        values_stage()

    def gd_parts(c):
        for y2 in range(4):
            yield y2, gin.at[c, :, pl.ds(y2 * 256, 256)], device(x, y2, z, t)

    def out_parts(c):
        for a in range(2):
            for t2 in range(2):
                to = (z, (2 * lax.rem(c, 2) + a) * 4 + y, t2)
                yield a * 2 + t2, gout.at[c, pl.ds(a * 32 + t2 * 16, 16), :], to

    def relay_step(c, carry):
        wait_bytes(gin.at[c], r_g.at[c])
        pbuf[c] = dot(gin[c], od[...], NT).astype(BF16)
        for k, x2, t2 in peers():
            push(
                pbuf.at[c, aligned(x2 * 16, 16), aligned(t2 * 256, 256)],
                rsb.at[c, k],
                s_rs.at[c],
                r_rs.at[c],
                device(x2, y, z, t2),
            )
        for k, src, to in gd_parts(c):
            send(src, gd.at[y, c], s_gd.at[c, k], r_gd, to)
        wait_bytes(rsb.at[c], r_rs.at[c])
        rows, cols = aligned(x * 16, 16), aligned(t * 256, 256)
        total = pbuf[c, rows, cols].astype(F32)
        for k in range(7):
            total = total + rsb[c, k].astype(F32)
        vg[y, c, rows, cols] = total.astype(BF16)
        mine = vg.at[y, c, rows, cols]
        for k, x2, t2 in peers():
            push(mine, mine, s_ag.at[c], r_ag.at[c], device(x2, y, z, t2))
        wait_bytes(rsb.at[c], r_ag.at[c])
        branch = dot(vg[y, c], vd[...], NT)
        gout[c] = (gin[c].astype(F32) + branch).astype(BF16)

        @pl.when(z > 0)
        def _():
            push(gout.at[c], gin.at[c], s_hop.at[c], r_g.at[c], device(x, y, z - 1, t))

        for k, src, to in out_parts(c):
            send(src, out.at[lax.div(c, 2), :, aligned(x * 2048 + t * 1024, 1024)], s_out.at[c, k], r_out, to)
        for k, y2 in y_peers():
            push(vg.at[y, c], vg.at[y, c], s_vg.at[c, k], r_vg, device(x, y2, z, t))
        return carry

    lax.fori_loop(0, CHUNKS, relay_step, 0)

    @pl.when(z >= 4)
    def _():
        values_stage()

    wait_bytes(xd, r_xd)
    wait_bytes(val.at[pl.ds(0, 3)], r_val)
    wait_bytes(gd, r_gd)
    wait_bytes(vg.at[pl.ds(0, 3)], r_vg)
    accv[...] = jnp.zeros_like(accv)
    acco[...] = jnp.zeros_like(acco)

    def grad_step(j, carry):
        accv[...] += dot(xd[j].reshape(512, 256), vg[j].reshape(512, 512), TN)
        acco[...] += dot(val[j], gd[j].reshape(512, 256), TN)
        return carry

    lax.fori_loop(0, 4, grad_step, 0)
    scale = 1.0 / math.sqrt(2048)
    for t2 in range(2):
        dvb[t2] = (accv[:, t2 * 256 : t2 * 256 + 256] * scale).astype(BF16)
        dob[t2, 0:16, :] = jnp.zeros((16, 256), BF16)
        dob[t2, 16:272, :] = (acco[t2 * 256 : t2 * 256 + 256, :] * scale).astype(BF16)
        dob[t2, 272:288, :] = jnp.zeros((16, 256), BF16)

    owner = 2 * x + t
    place = 8 * x + 4 * t + y

    def owner_parts(t2):
        yield 0, dvb.at[t2], vwin.at[pl.ds(pl.multiple_of(128 + y * 256, 128), 256)], 0, (z, owner, t2), None
        yield 1, dvb.at[t2, pl.ds(128, 128)], vwin.at[pl.ds(0, 128)], 1, (z, owner + 1, t2), y == 3
        yield 2, dvb.at[t2, pl.ds(0, 128)], vwin.at[pl.ds(1152, 128)], 2, (z, owner - 1, t2), jnp.logical_and(
            y == 0, owner >= 1
        )
        for k in range(8):
            yield 3 + k, dob.at[t2, pl.ds(32 * k, 64)], owin.at[place], 3, (z, 8 + k, t2), None
        yield 11, dob.at[t2, pl.ds(16, 16)], owin.at[place, pl.ds(48, 16)], 3, (z, 7, t2), None

    def guarded(cond, what):
        if cond is None:
            what()
        else:
            pl.when(cond)(what)

    for t2 in range(2):
        for k, src, dst, r, to, cond in owner_parts(t2):
            guarded(cond, functools.partial(send, src, dst, s_own.at[t2, k], r_own.at[r], to))

    @pl.when(dp <= 7)
    def _():
        wait_bytes(vwin.at[pl.ds(128, 1024)], r_own.at[0])

    @pl.when(jnp.logical_and(dp >= 1, dp <= 8))
    def _():
        wait_bytes(vwin.at[pl.ds(0, 128)], r_own.at[1])

    @pl.when(dp <= 6)
    def _():
        wait_bytes(vwin.at[pl.ds(1152, 128)], r_own.at[2])

    @pl.when(dp == 7)
    def _():
        wait_bytes(owin.at[pl.ds(0, 8)], r_own.at[3])

    @pl.when(dp >= 8)
    def _():
        wait_bytes(owin, r_own.at[3])

    wait_bytes(out, r_out)

    sent(vw, s_w1.at[0], w1_to)
    sent(ow, s_w1.at[1], w1_to)

    @pl.when(top_sender)
    def _():
        for k, src, c, to in top_parts():
            sent(src, s_top.at[k], to)

    for k, src, to in x_parts():
        sent(src, s_x.at[k], to)
    for k, src, dst, r, to in w2_parts():
        sent(src, s_w2.at[k], to)
    for k, src, to in xd_parts():
        sent(src, s_xd.at[k], to)
    wait_bytes(rsv, s_rsv)
    wait_bytes(rsv, s_agv)
    for k, y2 in y_peers():
        wait_bytes(val.at[y], s_val.at[k])

    def drain(c, carry):
        wait_bytes(rsb.at[c], s_rs.at[c])
        wait_bytes(rsb.at[c], s_ag.at[c])
        for k, src, to in gd_parts(c):
            sent(src, s_gd.at[c, k], to)

        @pl.when(z > 0)
        def _():
            wait_bytes(gout.at[c], s_hop.at[c])

        for k, src, to in out_parts(c):
            sent(src, s_out.at[c, k], to)
        for k, y2 in y_peers():
            wait_bytes(vg.at[y, c], s_vg.at[c, k])
        return carry

    lax.fori_loop(0, CHUNKS, drain, 0)
    for t2 in range(2):
        for k, src, dst, r, to, cond in owner_parts(t2):
            guarded(cond, functools.partial(sent, src, s_own.at[t2, k], to))


def relay(xin, top, vw, ow):
    hbm = pl.BlockSpec(memory_space=pl.ANY)
    dma = pltpu.SemaphoreType.DMA
    return pl.pallas_call(
        relay_kernel,
        out_shape=(
            jax.ShapeDtypeStruct((4, 16, 8192), BF16),
            jax.ShapeDtypeStruct((1280, 256), BF16),
            jax.ShapeDtypeStruct((32, 64, 256), BF16),
        ),
        in_specs=[hbm] * 4,
        out_specs=(hbm, hbm, hbm),
        scratch_shapes=[
            pltpu.VMEM((CHUNKS, 64, 1024), BF16),
            pltpu.VMEM((CHUNKS, 64, 1024), BF16),
            pltpu.VMEM((4, 2, 64, 1024), BF16),
            pltpu.VMEM((512, 256), BF16),
            pltpu.VMEM((256, 512), BF16),
            pltpu.VMEM((1024, 512), BF16),
            pltpu.VMEM((512, 1024), BF16),
            pltpu.VMEM((CHUNKS, 64, 512), BF16),
            pltpu.VMEM((CHUNKS, 7, 16, 256), BF16),
            pltpu.VMEM((4, CHUNKS, 64, 512), BF16),
            pltpu.VMEM((4, CHUNKS, 64, 256), BF16),
            pltpu.VMEM((512, 512), BF16),
            pltpu.VMEM((7, 128, 256), BF16),
            pltpu.VMEM((4, 512, 512), BF16),
            pltpu.VMEM((4, 4, 2, 64, 256), BF16),
            pltpu.VMEM((256, 512), F32),
            pltpu.VMEM((512, 256), F32),
            pltpu.VMEM((2, 256, 256), BF16),
            pltpu.VMEM((2, 288, 256), BF16),
            dma((8,)), dma((2,)), dma((8,)), dma((8,)),
            dma((CHUNKS,)), dma((CHUNKS,)), dma((CHUNKS,)), dma((CHUNKS, 4)),
            dma((CHUNKS, 4)), dma((CHUNKS, 3)), dma, dma,
            dma((3,)), dma((4,)), dma((2, 12)),
            dma, dma((2,)), dma((2,)), dma((CHUNKS,)),
            dma((CHUNKS,)), dma((CHUNKS,)), dma, dma, dma, dma,
            dma, dma, dma((4,)), dma,
        ],
        compiler_params=pltpu.CompilerParams(has_side_effects=True, vmem_limit_bytes=48 * 1024 * 1024),
    )(xin, top, vw, ow)


def adam_kernel(steps, lengths, vwin, owin, param, first, second, new_param, new_first, new_second, flat):
    dp = lax.axis_index("dp")
    step = pl.program_id(0)
    rows = param.shape[0]

    def from_value(low, high):
        for a in range(low, high, 128):
            part = vwin[a : a + 128, :].astype(F32)
            flat[pl.ds(2 * a, 128, stride=2), :] = part[:, :128]
            flat[pl.ds(2 * a + 1, 128, stride=2), :] = part[:, 128:]

    def from_output(low, high):
        for e in range(32):
            part = owin[e].astype(F32)[12 + low : 12 + high, :]
            for h in range(2):
                flat[pl.ds(low * 64 + e * 2 + h, high - low, stride=64), :] = part[:, h * 128 : h * 128 + 128]

    @pl.when(step == 0)
    def _():
        flat[2560:, :] = jnp.zeros((flat.shape[0] - 2560, 128), F32)
        for last, value_rows, output_rows in ((8, (0, 128), (0, 4)), (7, (128, 1152), (4, 36)), (6, (1152, 1280), (36, 40))):
            pl.when(dp <= last)(functools.partial(from_value, *value_rows))
            pl.when(dp > last)(functools.partial(from_output, *output_rows))

    start = lax.fori_loop(0, dp, lambda e, total: total + lengths[e], jnp.int32(0))
    length = lengths[dp]
    offset = start - dp * 262144 + 32768
    row, lane = lax.div(offset, 128), lax.rem(offset, 128)
    window = flat[pl.ds(step * rows + row, rows + 8), :]
    turned = pltpu.roll(window, lax.rem(128 - lane, 128), 1)
    lanes = lax.broadcasted_iota(jnp.int32, (rows, 128), 1)
    grad = jnp.where(lanes < 128 - lane, turned[:rows], turned[1 : rows + 1])
    index = (step * rows + lax.broadcasted_iota(jnp.int32, (rows, 128), 0)) * 128 + lanes
    grad = jnp.where(index < length, grad, 0.0)

    first_new = beta_one * first[...] + (1.0 - beta_one) * grad
    second_new = beta_two * second[...] + (1.0 - beta_two) * grad * grad
    corrected = (
        first_new
        / (1.0 - beta_one**adam_step)
        / (jnp.sqrt(second_new / (1.0 - beta_two**adam_step)) + adam_eps)
    )
    new_param[...] = param[...] - learn_rate * (corrected + decay_rate * param[...])
    new_first[...] = first_new
    new_second[...] = second_new


def adam(lengths, vwin, owin, param, first, second):
    steps = 5
    block = pl.BlockSpec((2560 // steps, 128), lambda i: (i, 0))
    shape = jax.ShapeDtypeStruct((2560, 128), F32)
    return pl.pallas_call(
        functools.partial(adam_kernel, steps),
        grid=(steps,),
        out_shape=(shape, shape, shape),
        in_specs=[
            pl.BlockSpec(memory_space=pltpu.SMEM),
            pl.BlockSpec(memory_space=pltpu.VMEM),
            pl.BlockSpec(memory_space=pltpu.VMEM),
            block,
            block,
            block,
        ],
        out_specs=(block, block, block),
        scratch_shapes=[pltpu.VMEM((2560 + 528, 128), F32)],
        compiler_params=pltpu.CompilerParams(vmem_limit_bytes=32 * 1024 * 1024),
    )(lengths, vwin, owin, param, first, second)


def local(section_inputs, top_grad, value_weight, output_weight, owner_lengths, master_param, moment1, moment2):
    out, vwin, owin = relay(section_inputs[0], top_grad, value_weight[0], output_weight[0])
    flat = (2560, 128)
    updated = adam(
        owner_lengths[0, 0], vwin, owin, master_param.reshape(flat), moment1.reshape(flat), moment2.reshape(flat)
    )
    return (out[None], *(array.reshape(1, 1, -1) for array in updated))


def solution(mesh):
    in_specs = (
        P("section", None, ("dp", "tensor"), None),
        P(None, ("dp", "tensor"), None),
        P("section", "dp", "tensor"),
        P("section", "tensor", "dp"),
        P("section", "tensor", None),
        P("section", "tensor", "dp"),
        P("section", "tensor", "dp"),
        P("section", "tensor", "dp"),
    )
    out_specs = (
        P("section", None, ("dp", "tensor"), None),
        P("section", "tensor", "dp"),
        P("section", "tensor", "dp"),
        P("section", "tensor", "dp"),
    )
    return jax.shard_map(local, mesh=mesh, in_specs=in_specs, out_specs=out_specs, check_vma=False)
```

time: 1820 us -> 408 us (0.22)
  waiting for transfers between devices: 1120 us -> 0 us
  local copies, waits for them, and re-layouts: 427 us -> 6.63 us
  Pallas kernels: 0 us -> 400 us
  other arithmetic: 123 us -> 0 us
  matrix products: 75.2 us -> 0 us
  loops' own time: 31.8 us -> 0 us
    psum x11 -> x0, waiting for transfers between devices: 482 us -> none  [step_body(): summed = lax.psum(branch.astype(jnp.bfloat16), 'tensor').astype(jnp.float32)]
    pallas_call x0 -> x2, Pallas kernels: none -> 400 us  [the longest x1 395 us: relay(): pl.pallas_call(relay_kernel, out_shape=(jax.ShapeDtypeStruct((4, 16, 8192...]
    dynamic_update_slice x16 -> x0, local copies, waits for them, and re-layouts: 385 us -> none  [owner_slices(): return lax.map(take_one, (starts, lengths))]
    unnamed x6 -> x0, waiting for transfers between devices: 257 us -> none
    all_gather x4 -> x0, waiting for transfers between devices: 202 us -> none  [the longest x1 88.2 us: local(): lax.all_gather(output_weight[0], 'dp', axis=1, tiled=True)]
    ppermute x11 -> x0, waiting for transfers between devices: 177 us -> none  [shifted(): return lax.ppermute(block, axis, route)]
    dot_general x24 -> x0, matrix products: 75.2 us -> none  [the longest x11 40.6 us: step_body(): lax.dot_general(arrived, output_full, contract, preferred_element_type=jn...]
    select_n x38 -> x0, other arithmetic: 71 us -> none  [the longest x16 38 us: take_one(): return jnp.where(offsets < length, piece, jnp.zeros((), flat_grad.dtype))]
  transfers between devices with their start and end apart: 27 -> 0, of which waited for: 27 -> 0; matrix products, arithmetic and copies ran while one was open for 1% -> 0% of each run, Pallas kernels for 0% -> 0%
where the time goes in v1:
time: 408 us
  Pallas kernels  400 us (98%)
  local copies, waits for them, and re-layouts  6.63 us (2%)
    pallas_call x1, Pallas kernels, relay(): pl.pallas_call(relay_kernel, out_shape=(jax.ShapeDtypeStruct((4, 16, 8192...  395 us

profile of v1, /device:TPU:97, one launch (start us, length us, event | category | flops | bytes accessed | tf_op | source)
XLA Modules:
  0.0 407.6 jit_solution(2526985940481294832)
XLA Ops:
  0.6 0.0 copy-start.3
  0.6 1.2 copy-done.3
  1.9 0.0 copy-start.4
  1.9 1.2 copy-done.4
  3.1 0.0 copy-start.5
  3.1 0.9 copy-done.5
  4.0 0.0 copy-start.6
  4.0 0.9 copy-done.6
  5.0 0.0 copy-start
  5.0 0.0 copy-start.1
  5.0 0.0 copy-start.7
  5.0 394.7 %shard_map.111 = (bf16[4,16,8192]{2,1,0:T(8,128)(2,1)S(1)}, bf16[1280,256]{1,0:T(8,128)(2,1)S(1)}, bf16[32,64,256]{2,1,0:T(8,128)(2,1)S(1)}) custom-call(bf16[4,16,8192]{2,1,0:T(8,128)(2,1)S(1)} %bitcast.14, bf16[4,16,8192]{2,1,0:T(8,128)(2,1)S(1)} %copy-done.4, bf16[512,256]{1,0:T(8,128)(2,1)S(1)} %bitcast.16, bf16[256,512]{1,0:T(8,128)(2,1)S(1)} %bitcast.17), custom_call_target="tpu_custom_call" | custom-call | tf_op jit(solution)/shard_map/pallas_call | solution.py:330
  399.7 0.0 copy-done
  399.7 0.0 copy-done.1
  399.7 0.0 copy-done.7
  399.8 0.0 copy-start.2
  399.8 1.3 copy-done.2
  401.1 5.6 %shard_map.112 = (f32[2560,128]{1,0:T(8,128)}, f32[2560,128]{1,0:T(8,128)}, f32[2560,128]{1,0:T(8,128)}) custom-call(s32[16]{0:T(128)S(1)} %bitcast.18, bf16[1280,256]{1,0:T(8,128)(2,1)S(1)} %get-tuple-element.11.vwin, bf16[32,64,256]{2,1,0:T(8,128)(2,1)S(1)} %get-tuple-element.12.owin, f32[2560,128]{1,0:T(8,128)S(1)} %bitcast.11, f32[2560,128]{1,0:T(8,128)S(1)} %bitcast.12, ...), custom_call_target="tpu_custom_call" | custom-call | tf_op jit(solution)/shard_map/pallas_call | solution.py:422
  406.6 1.0 copy.13
Async XLA Ops:
  0.6 1.2 copy-start.3
  1.9 1.2 copy-start.4
  3.1 0.9 copy-start.5
  4.0 0.9 copy-start.6
  5.0 394.7 %copy-start = (f32[1,1,327680]{2,1,0:T(1,128)S(1)}, f32[1,1,327680]{2,1,0:T(1,128)}, u32[]{:S(2)}) copy-start(f32[1,1,327680]{2,1,0:T(1,128)} %param.13) | copy-start | bytes 3932164
  5.0 394.8 %copy-start.1 = (f32[1,1,327680]{2,1,0:T(1,128)S(1)}, f32[1,1,327680]{2,1,0:T(1,128)}, u32[]{:S(2)}) copy-start(f32[1,1,327680]{2,1,0:T(1,128)} %param.14) | copy-start | bytes 3932164
  5.0 394.8 %copy-start.7 = (s32[1,1,16]{2,1,0:T(1,128)S(1)}, s32[1,1,16]{2,1,0:T(1,128)}, u32[]{:S(2)}) copy-start(s32[1,1,16]{2,1,0:T(1,128)} %param.12) | copy-start | bytes 196
  399.8 1.3 copy-start.2

commit v2 on v1

--- a/solution.py
+++ b/solution.py
@@ -44,9 +44,9 @@
 def relay_kernel(
     xin, top, vw, ow,
     out, vwin, owin,
-    gin, gout, xrow, vst, ost, vd, od, pbuf, rsb, vg, gd, pv, rsv, val, xd, accv, acco, dvb, dob,
-    s_x, s_w1, s_w2, s_top, s_rs, s_ag, s_hop, s_out, s_gd, s_vg, s_rsv, s_agv, s_val, s_xd, s_own,
-    r_x, r_w1, r_w2, r_g, r_rs, r_ag, r_gd, r_vg, r_rsv, r_agv, r_val, r_xd, r_own, r_out,
+    gin, gout, xrow, xst, vwst, owst, vst, ost, vd, od, pbuf, rsb, vg, gd, pv, rsv, val, xd, accv, acco, dvb, dob,
+    s_xa, s_x, s_wa, s_w1, s_w2, s_top, s_rs, s_ag, s_hop, s_out, s_gd, s_vg, s_rsv, s_agv, s_val, s_xd, s_own,
+    r_xa, r_x, r_wa, r_w1, r_w2, r_g, r_rs, r_ag, r_gd, r_vg, r_rsv, r_agv, r_val, r_xd, r_own, r_out,
 ):
     sec = lax.axis_index("section")
     dp = lax.axis_index("dp")
@@ -78,9 +78,10 @@
     def push(src, dst, ssem, rsem, to):
         pltpu.make_async_remote_copy(src, dst, ssem, rsem, device_id=to, device_id_type=MESH).start()
 
-    w1_to = device(zl, y, sec, t)
-    send(vw, vst, s_w1.at[0], r_w1.at[0], w1_to)
-    send(ow, ost, s_w1.at[1], r_w1.at[1], w1_to)
+    zh = lax.rem(sec, 2)
+    wa_to = device(zl, y, z, t)
+    send(vw, vwst.at[x], s_wa.at[0], r_wa.at[x, 0], wa_to)
+    send(ow, owst.at[x], s_wa.at[1], r_wa.at[x, 1], wa_to)
 
     half = lax.div(zl, 2)
     row16 = aligned(lax.rem(zl, 2) * 32 + t * 16, 16)
@@ -98,16 +99,27 @@
             send(src, gin.at[c, row16, :], s_top.at[k], r_g.at[c], to)
 
     def x_parts():
-        for x2 in range(4):
+        for x2 in range(4 ):
             for t2 in range(2):
-                src = xin.at[:, :, pl.ds(x2 * 2048 + t2 * 1024, 1024)]
-                yield x2 * 2 + t2, src, device(x2, y, sec, t2)
-
-    for k, src, to in x_parts():
-        send(src, xrow.at[:, half, row16, :], s_x.at[k], r_x, to)
+                yield x2 * 2 + t2, xin.at[:, :, pl.ds(x2 * 2048 + t2 * 1024, 1024)], device(x2, y, z, t2)
+
+    def x_moves():
+        for x2 in reversed(range(4 )):
+            yield x2, xst.at[x2], device(x, y, 2 * x2 + zh, t)
+
+    @pl.when(x == zl)
+    def _():
+        for x2 in reversed(range(4)):
+            to = device(x, y, 2 * x2 + zh, t)
+            wait_bytes(vwst.at[x2], r_wa.at[x2, 0])
+            send(vwst.at[x2], vst, s_w1.at[x2, 0], r_w1.at[0], to)
+            wait_bytes(owst.at[x2], r_wa.at[x2, 1])
+            send(owst.at[x2], ost, s_w1.at[x2, 1], r_w1.at[1], to)
 
     wait_bytes(vst, r_w1.at[0])
     wait_bytes(ost, r_w1.at[1])
+    for k, src, to in x_parts():
+        send(src, xst.at[x, :, aligned(t * 16, 16), :], s_xa.at[k], r_xa.at[x], to)
 
     def w2_parts():
         rows = aligned(lax.rem(y, 2) * 512, 512)
@@ -121,6 +133,9 @@
         send(src, dst, s_w2.at[k], r_w2.at[r], to)
     wait_bytes(vd, r_w2.at[0])
     wait_bytes(od, r_w2.at[1])
+    for k, src, to in x_moves():
+        wait_bytes(src, r_xa.at[k])
+        send(src, xrow.at[:, half, aligned(lax.rem(zl, 2) * 32, 32), :], s_x.at[k], r_x, to)
 
     def peers():
         for k in range(1, 8):
@@ -162,7 +177,7 @@
         for k, y2 in y_peers():
             push(val.at[y], val.at[y], s_val.at[k], r_val, device(x, y2, z, t))
 
-    @pl.when(z < 4)
+    @pl.when(z < 3)
     def _():
         values_stage()
 
@@ -176,7 +191,7 @@
                 to = (z, (2 * lax.rem(c, 2) + a) * 4 + y, t2)
                 yield a * 2 + t2, gout.at[c, pl.ds(a * 32 + t2 * 16, 16), :], to
 
-    def relay_step(c, carry):
+    def first_part(c):
         wait_bytes(gin.at[c], r_g.at[c])
         pbuf[c] = dot(gin[c], od[...], NT).astype(BF16)
         for k, x2, t2 in peers():
@@ -189,6 +204,8 @@
             )
         for k, src, to in gd_parts(c):
             send(src, gd.at[y, c], s_gd.at[c, k], r_gd, to)
+
+    def second_part(c):
         wait_bytes(rsb.at[c], r_rs.at[c])
         rows, cols = aligned(x * 16, 16), aligned(t * 256, 256)
         total = pbuf[c, rows, cols].astype(F32)
@@ -198,6 +215,8 @@
         mine = vg.at[y, c, rows, cols]
         for k, x2, t2 in peers():
             push(mine, mine, s_ag.at[c], r_ag.at[c], device(x2, y, z, t2))
+
+    def third_part(c):
         wait_bytes(rsb.at[c], r_ag.at[c])
         branch = dot(vg[y, c], vd[...], NT)
         gout[c] = (gin[c].astype(F32) + branch).astype(BF16)
@@ -210,11 +229,21 @@
             send(src, out.at[lax.div(c, 2), :, aligned(x * 2048 + t * 1024, 1024)], s_out.at[c, k], r_out, to)
         for k, y2 in y_peers():
             push(vg.at[y, c], vg.at[y, c], s_vg.at[c, k], r_vg, device(x, y2, z, t))
+
+    def relay_step(c, carry):
+        second_part(c)
+
+        @pl.when(c + 1 < CHUNKS)
+        def _():
+            first_part(c + 1)
+
+        third_part(c)
         return carry
 
+    first_part(0)
     lax.fori_loop(0, CHUNKS, relay_step, 0)
 
-    @pl.when(z >= 4)
+    @pl.when(z >= 3)
     def _():
         values_stage()
 
@@ -283,8 +312,18 @@
 
     wait_bytes(out, r_out)
 
-    sent(vw, s_w1.at[0], w1_to)
-    sent(ow, s_w1.at[1], w1_to)
+    sent(vw, s_wa.at[0], wa_to)
+    sent(ow, s_wa.at[1], wa_to)
+
+    @pl.when(x == zl)
+    def _():
+        for x2 in range(4):
+            to = device(x, y, 2 * x2 + zh, t)
+            sent(vst, s_w1.at[x2, 0], to)
+            sent(ost, s_w1.at[x2, 1], to)
+
+    for k, src, to in x_moves():
+        sent(src, s_x.at[k], to)
 
     @pl.when(top_sender)
     def _():
@@ -292,7 +331,7 @@
             sent(src, s_top.at[k], to)
 
     for k, src, to in x_parts():
-        sent(src, s_x.at[k], to)
+        sent(src, s_xa.at[k], to)
     for k, src, dst, r, to in w2_parts():
         sent(src, s_w2.at[k], to)
     for k, src, to in xd_parts():
@@ -340,6 +379,9 @@
             pltpu.VMEM((CHUNKS, 64, 1024), BF16),
             pltpu.VMEM((CHUNKS, 64, 1024), BF16),
             pltpu.VMEM((4, 2, 64, 1024), BF16),
+            pltpu.VMEM((4, 4, 32, 1024), BF16),
+            pltpu.VMEM((4, 512, 256), BF16),
+            pltpu.VMEM((4, 256, 512), BF16),
             pltpu.VMEM((512, 256), BF16),
             pltpu.VMEM((256, 512), BF16),
             pltpu.VMEM((1024, 512), BF16),
@@ -356,11 +398,11 @@
             pltpu.VMEM((512, 256), F32),
             pltpu.VMEM((2, 256, 256), BF16),
             pltpu.VMEM((2, 288, 256), BF16),
-            dma((8,)), dma((2,)), dma((8,)), dma((8,)),
+            dma((8,)), dma((4,)), dma((2,)), dma((4, 2)), dma((8,)), dma((8,)),
             dma((CHUNKS,)), dma((CHUNKS,)), dma((CHUNKS,)), dma((CHUNKS, 4)),
             dma((CHUNKS, 4)), dma((CHUNKS, 3)), dma, dma,
             dma((3,)), dma((4,)), dma((2, 12)),
-            dma, dma((2,)), dma((2,)), dma((CHUNKS,)),
+            dma((4,)), dma, dma((4, 2)), dma((2,)), dma((2,)), dma((CHUNKS,)),
             dma((CHUNKS,)), dma((CHUNKS,)), dma, dma, dma, dma,
             dma, dma, dma((4,)), dma,
         ],

time: 408 us -> 306 us (0.75)
  Pallas kernels: 400 us -> 298 us
    pallas_call x1, Pallas kernels: 395 us -> 292 us  [relay(): pl.pallas_call(relay_kernel, out_shape=(jax.ShapeDtypeStruct((4, 16, 8192...]
where the time goes in v2:
time: 306 us; the launch traced here: 305 us
  Pallas kernels  298 us (97%)
  local copies, waits for them, and re-layouts  6.63 us (2%)
    pallas_call x1, Pallas kernels, relay(): pl.pallas_call(relay_kernel, out_shape=(jax.ShapeDtypeStruct((4, 16, 8192...  292 us
    unnamed x17, local copies, waits for them, and re-layouts  6.63 us

profile of v2, /device:TPU:97, one launch (start us, length us, event | category | flops | bytes accessed | tf_op | source)
XLA Modules:
  0.0 305.1 jit_solution(15496413853060681060)
XLA Ops:
  0.6 0.0 copy-start.3
  0.6 1.2 copy-done.3
  1.9 0.0 copy-start.4
  1.9 1.2 copy-done.4
  3.1 0.0 copy-start.5
  3.1 0.9 copy-done.5
  4.0 0.0 copy-start.6
  4.0 0.9 copy-done.6
  5.0 0.0 copy-start
  5.0 0.0 copy-start.1
  5.0 0.0 copy-start.7
  5.0 292.2 %shard_map.111 = (bf16[4,16,8192]{2,1,0:T(8,128)(2,1)S(1)}, bf16[1280,256]{1,0:T(8,128)(2,1)S(1)}, bf16[32,64,256]{2,1,0:T(8,128)(2,1)S(1)}) custom-call(bf16[4,16,8192]{2,1,0:T(8,128)(2,1)S(1)} %bitcast.14, bf16[4,16,8192]{2,1,0:T(8,128)(2,1)S(1)} %copy-done.4, bf16[512,256]{1,0:T(8,128)(2,1)S(1)} %bitcast.16, bf16[256,512]{1,0:T(8,128)(2,1)S(1)} %bitcast.17), custom_call_target="tpu_custom_call" | custom-call | tf_op jit(solution)/shard_map/pallas_call | solution.py:369
  297.2 0.0 copy-done
  297.2 0.0 copy-done.1
  297.2 0.0 copy-done.7
  297.2 0.0 copy-start.2
  297.2 1.3 copy-done.2
  298.5 5.6 %shard_map.112 = (f32[2560,128]{1,0:T(8,128)}, f32[2560,128]{1,0:T(8,128)}, f32[2560,128]{1,0:T(8,128)}) custom-call(s32[16]{0:T(128)S(1)} %bitcast.18, bf16[1280,256]{1,0:T(8,128)(2,1)S(1)} %get-tuple-element.11.vwin, bf16[32,64,256]{2,1,0:T(8,128)(2,1)S(1)} %get-tuple-element.12.owin, f32[2560,128]{1,0:T(8,128)S(1)} %bitcast.11, f32[2560,128]{1,0:T(8,128)S(1)} %bitcast.12, ...), custom_call_target="tpu_custom_call" | custom-call | tf_op jit(solution)/shard_map/pallas_call | solution.py:464
  304.1 1.0 copy.13
Async XLA Ops:
  0.6 1.2 copy-start.3
  1.9 1.2 copy-start.4
  3.1 0.9 copy-start.5
  4.0 0.9 copy-start.6
  5.0 292.2 %copy-start = (f32[1,1,327680]{2,1,0:T(1,128)S(1)}, f32[1,1,327680]{2,1,0:T(1,128)}, u32[]{:S(2)}) copy-start(f32[1,1,327680]{2,1,0:T(1,128)} %param.13) | copy-start | bytes 3932164
  5.0 292.2 %copy-start.1 = (f32[1,1,327680]{2,1,0:T(1,128)S(1)}, f32[1,1,327680]{2,1,0:T(1,128)}, u32[]{:S(2)}) copy-start(f32[1,1,327680]{2,1,0:T(1,128)} %param.14) | copy-start | bytes 3932164
  5.0 292.2 %copy-start.7 = (s32[1,1,16]{2,1,0:T(1,128)S(1)}, s32[1,1,16]{2,1,0:T(1,128)}, u32[]{:S(2)}) copy-start(s32[1,1,16]{2,1,0:T(1,128)} %param.12) | copy-start | bytes 196
  297.2 1.3 copy-start.2

commit v3 on v1

--- a/solution.py
+++ b/solution.py
@@ -20,6 +20,9 @@
 adam_step = 20.0
 
 CHUNKS = 8
+ROWS = 512 // CHUNKS
+PIECE = ROWS // 4
+MOVE_AT = 2
 NT = (((1,), (1,)), ((), ()))
 NN = (((1,), (0,)), ((), ()))
 TN = (((0,), (0,)), ((), ()))
@@ -44,17 +47,22 @@
 def relay_kernel(
     xin, top, vw, ow,
     out, vwin, owin,
-    gin, gout, xrow, vst, ost, vd, od, pbuf, rsb, vg, gd, pv, rsv, val, xd, accv, acco, dvb, dob,
-    s_x, s_w1, s_w2, s_top, s_rs, s_ag, s_hop, s_out, s_gd, s_vg, s_rsv, s_agv, s_val, s_xd, s_own,
-    r_x, r_w1, r_w2, r_g, r_rs, r_ag, r_gd, r_vg, r_rsv, r_agv, r_val, r_xd, r_own, r_out,
+    gtop, gin, gout, xrow, xst, vwst, owst, vst, ost, vd, od, pbuf, rsb, vgo, vg, gd, pv, rsv, val, xd,
+    accv, acco, dvb, dob, mid,
+    s_xa, s_x, s_wa, s_w1, s_w2, s_top, s_rs, s_ag, s_hop, s_out, s_gd, s_vg, s_rsv, s_agv, s_val, s_xd,
+    s_own, s_mid, s_fin,
+    r_xa, r_x, r_wa, r_w1, r_w2, r_top, r_g, r_rs, r_ag, r_gd, r_vg, r_rsv, r_agv, r_val, r_xd, r_own, r_mid, r_out,
 ):
     sec = lax.axis_index("section")
     dp = lax.axis_index("dp")
     t = lax.axis_index("tensor")
     x = lax.div(sec, 2)
+    zh = lax.rem(sec, 2)
     zl = lax.div(dp, 4)
     y = lax.rem(dp, 4)
-    z = lax.rem(sec, 2) * 4 + zl
+    z = zh * 4 + zl
+    after = lax.rem(z + 1, 8)
+    below = lax.rem(z + 7, 8)
 
     def is_me(to):
         return jnp.logical_and(jnp.logical_and(to[0] == sec, to[1] == dp), to[2] == t)
@@ -78,48 +86,71 @@
     def push(src, dst, ssem, rsem, to):
         pltpu.make_async_remote_copy(src, dst, ssem, rsem, device_id=to, device_id_type=MESH).start()
 
-    w1_to = device(zl, y, sec, t)
-    send(vw, vst, s_w1.at[0], r_w1.at[0], w1_to)
-    send(ow, ost, s_w1.at[1], r_w1.at[1], w1_to)
-
-    half = lax.div(zl, 2)
-    row16 = aligned(lax.rem(zl, 2) * 32 + t * 16, 16)
-    top_sender = jnp.logical_or(z < 2, z >= 6)
+    wa_to = device(zl, y, z, t)
+    send(ow, owst.at[x], s_wa.at[1], r_wa.at[x, 1], wa_to)
 
     def top_parts():
         for mb in range(4):
             for t2 in range(2):
+                row = mb * 128 + zl * 32 + t * 16
+                c, rest = lax.div(row, ROWS), lax.rem(row, ROWS)
                 src = top.at[mb, :, aligned(x * 2048 + t2 * 1024, 1024)]
-                yield mb * 2 + t2, src, mb * 2 + half, device(x, y, 7, t2)
+                yield mb * 2 + t2, src, gtop.at[c, aligned(rest, 16), :], c, device(x, y, 7, t2)
+
+    top_sender = jnp.logical_or(z < 2, z >= 6)
 
     @pl.when(top_sender)
     def _():
-        for k, src, c, to in top_parts():
-            send(src, gin.at[c, row16, :], s_top.at[k], r_g.at[c], to)
-
-    def x_parts():
-        for x2 in range(4):
-            for t2 in range(2):
-                src = xin.at[:, :, pl.ds(x2 * 2048 + t2 * 1024, 1024)]
-                yield x2 * 2 + t2, src, device(x2, y, sec, t2)
-
-    for k, src, to in x_parts():
-        send(src, xrow.at[:, half, row16, :], s_x.at[k], r_x, to)
-
-    wait_bytes(vst, r_w1.at[0])
-    wait_bytes(ost, r_w1.at[1])
-
-    def w2_parts():
+        for k, src, dst, c, to in top_parts():
+            send(src, dst, s_top.at[k], r_top.at[c], to)
+
+    send(vw, vwst.at[x], s_wa.at[0], r_wa.at[x, 0], wa_to)
+
+    def w1_parts(which):
+        for x2 in reversed(range(4)):
+            plane = 2 * x2 + zh
+            if which:
+                yield x2, owst.at[x2], ost, device(x, y, plane, t)
+            else:
+                yield x2, vwst.at[x2], vst, device(x, y, lax.rem(plane + 7, 8), t)
+
+    def w2_parts(which):
         rows = aligned(lax.rem(y, 2) * 512, 512)
         cols = aligned(t * 256, 256)
         for y2 in range(4):
             to = device(x, y2, z, lax.div(y, 2))
-            yield y2, vst, vd.at[rows, cols], 0, to
-            yield 4 + y2, ost, od.at[cols, rows], 1, to
-
-    for k, src, dst, r, to in w2_parts():
-        send(src, dst, s_w2.at[k], r_w2.at[r], to)
-    wait_bytes(vd, r_w2.at[0])
+            if which:
+                yield y2, ost, od.at[cols, rows], to
+            else:
+                yield y2, vst, vd.at[rows, cols], to
+
+    def x_parts():
+        for x2 in range(4):
+            for t2 in range(2):
+                yield x2 * 2 + t2, xin.at[:, :, pl.ds(x2 * 2048 + t2 * 1024, 1024)], device(x2, y, z, t2)
+
+    def x_moves():
+        for x2 in reversed(range(4)):
+            yield x2, xst.at[x2], device(x, y, lax.rem(2 * x2 + zh + 7, 8), t)
+
+    def move_inputs():
+        for k, src, to in x_moves():
+            wait_bytes(src, r_xa.at[k])
+            send(src, xrow.at[:, aligned(zl * 32, 32), :], s_x.at[k], r_x, to)
+
+    for which in (1, 0):
+
+        @pl.when(x == zl)
+        def _():
+            for k, src, dst, to in w1_parts(which):
+                wait_bytes(src, r_wa.at[k, which])
+                send(src, dst, s_w1.at[k, which], r_w1.at[which], to)
+
+        wait_bytes(ost if which else vst, r_w1.at[which])
+        for k, src, dst, to in w2_parts(which):
+            send(src, dst, s_w2.at[k, which], r_w2.at[which], to)
+    for k, src, to in x_parts():
+        send(src, xst.at[x, :, aligned(t * 16, 16), :], s_xa.at[k], r_xa.at[x], to)
     wait_bytes(od, r_w2.at[1])
 
     def peers():
@@ -130,9 +161,56 @@
         for k in range(1, 4):
             yield k - 1, lax.rem(y + k, 4)
 
+    def multiply(ref, c):
+        pbuf[c] = dot(ref[c], od[...], NT).astype(BF16)
+        for k, x2, t2 in peers():
+            push(
+                pbuf.at[c, aligned(x2 * PIECE, PIECE), aligned(t2 * 256, 256)],
+                rsb.at[c, k],
+                s_rs.at[c],
+                r_rs.at[c],
+                device(x2, y, z, t2),
+            )
+
+    def add_up(c):
+        rows, cols = aligned(x * PIECE, PIECE), aligned(t * 256, 256)
+        wait_bytes(rsb.at[c], r_rs.at[c])
+        total = pbuf[c, rows, cols].astype(F32)
+        for k in range(7):
+            total = total + rsb[c, k].astype(F32)
+        vgo[c] = total.astype(BF16)
+        for k in range(8):
+            to = device(lax.rem(x + k // 2, 4), y, below, lax.rem(t + k % 2, 2))
+            push(vgo.at[c], vg.at[y, c, rows, cols], s_ag.at[c], r_ag.at[c], to)
+
+    def add_branch(c):
+        wait_bytes(gin.at[c], r_g.at[c])
+        wait_bytes(vg.at[y, c], r_ag.at[c])
+        branch = dot(vg[y, c], vd[...], NT)
+        gout[c] = (gin[c].astype(F32) + branch).astype(BF16)
+
+    def gd_parts(c):
+        for y2 in range(4):
+            yield y2, gin.at[c, :, pl.ds(y2 * 256, 256)], device(x, y2, z, t)
+
+    def out_parts(c):
+        for a in range(ROWS // 16):
+            row = c * ROWS + a * 16
+            mb, z2, t2 = lax.div(row, 128), lax.rem(lax.div(row, 32), 4), a % 2
+            dst = out.at[mb, :, aligned(x * 2048 + t * 1024, 1024)]
+            yield a, gout.at[c, pl.ds(a * 16, 16), :], dst, (after, z2 * 4 + y, t2)
+
+    def hand_out(c):
+        for k, src, dst, to in out_parts(c):
+            send(src, dst, s_out.at[c, k], r_out, to)
+        for k, y2 in y_peers():
+            push(vg.at[y, c], vg.at[y, c], s_vg.at[c, k], r_vg, device(x, y2, z, t))
+        for k, src, to in gd_parts(c):
+            send(src, gd.at[y, c], s_gd.at[c, k], r_gd, to)
+
     def xd_parts():
         for y2 in range(4):
-            yield y2, xrow.at[:, :, :, pl.ds(y2 * 256, 256)], device(x, y2, z, t)
+            yield y2, xrow.at[:, :, pl.ds(y2 * 256, 256)], device(x, y2, z, t)
 
     def values_stage():
         wait_bytes(xrow, r_x)
@@ -140,11 +218,10 @@
             send(src, xd.at[y], s_xd.at[k], r_xd, to)
 
         def block(i, carry):
-            rows = xrow[lax.div(i, 2), lax.rem(i, 2)]
-            pv[aligned(i * 64, 64), :] = dot(rows, vd[...], NN).astype(BF16)
+            pv[aligned(i * 128, 128), :] = dot(xrow[i], vd[...], NN).astype(BF16)
             return carry
 
-        lax.fori_loop(0, 8, block, 0)
+        lax.fori_loop(0, 4, block, 0)
         for k, x2, t2 in peers():
             push(
                 pv.at[aligned(x2 * 128, 128), aligned(t2 * 256, 256)], rsv.at[k], s_rsv, r_rsv, device(x2, y, z, t2)
@@ -162,61 +239,49 @@
         for k, y2 in y_peers():
             push(val.at[y], val.at[y], s_val.at[k], r_val, device(x, y2, z, t))
 
-    @pl.when(z < 4)
-    def _():
-        values_stage()
-
-    def gd_parts(c):
-        for y2 in range(4):
-            yield y2, gin.at[c, :, pl.ds(y2 * 256, 256)], device(x, y2, z, t)
-
-    def out_parts(c):
-        for a in range(2):
-            for t2 in range(2):
-                to = (z, (2 * lax.rem(c, 2) + a) * 4 + y, t2)
-                yield a * 2 + t2, gout.at[c, pl.ds(a * 32 + t2 * 16, 16), :], to
-
-    def relay_step(c, carry):
-        wait_bytes(gin.at[c], r_g.at[c])
-        pbuf[c] = dot(gin[c], od[...], NT).astype(BF16)
-        for k, x2, t2 in peers():
-            push(
-                pbuf.at[c, aligned(x2 * 16, 16), aligned(t2 * 256, 256)],
-                rsb.at[c, k],
-                s_rs.at[c],
-                r_rs.at[c],
-                device(x2, y, z, t2),
-            )
-        for k, src, to in gd_parts(c):
-            send(src, gd.at[y, c], s_gd.at[c, k], r_gd, to)
-        wait_bytes(rsb.at[c], r_rs.at[c])
-        rows, cols = aligned(x * 16, 16), aligned(t * 256, 256)
-        total = pbuf[c, rows, cols].astype(F32)
-        for k in range(7):
-            total = total + rsb[c, k].astype(F32)
-        vg[y, c, rows, cols] = total.astype(BF16)
-        mine = vg.at[y, c, rows, cols]
-        for k, x2, t2 in peers():
-            push(mine, mine, s_ag.at[c], r_ag.at[c], device(x2, y, z, t2))
-        wait_bytes(rsb.at[c], r_ag.at[c])
-        branch = dot(vg[y, c], vd[...], NT)
-        gout[c] = (gin[c].astype(F32) + branch).astype(BF16)
-
-        @pl.when(z > 0)
-        def _():
-            push(gout.at[c], gin.at[c], s_hop.at[c], r_g.at[c], device(x, y, z - 1, t))
-
-        for k, src, to in out_parts(c):
-            send(src, out.at[lax.div(c, 2), :, aligned(x * 2048 + t * 1024, 1024)], s_out.at[c, k], r_out, to)
-        for k, y2 in y_peers():
-            push(vg.at[y, c], vg.at[y, c], s_vg.at[c, k], r_vg, device(x, y2, z, t))
-        return carry
-
-    lax.fori_loop(0, CHUNKS, relay_step, 0)
-
-    @pl.when(z >= 4)
-    def _():
-        values_stage()
+    @pl.when(z == 7)
+    def _():
+        def begin(c):
+            wait_bytes(gtop.at[c], r_top.at[c])
+            push(gtop.at[c], gin.at[c], s_hop.at[c], r_g.at[c], device(x, y, below, t))
+            multiply(gtop, c)
+
+        def step(c, carry):
+            pl.when(c + 1 < CHUNKS)(lambda: begin(c + 1))
+            pl.when(c == MOVE_AT)(move_inputs)
+            add_up(c)
+            return carry
+
+        begin(0)
+        lax.fori_loop(0, CHUNKS, step, 0)
+        wait_bytes(vd, r_w2.at[0])
+
+    @pl.when(z < 7)
+    def _():
+        move_inputs()
+        wait_bytes(vd, r_w2.at[0])
+        pl.when(z < 2)(values_stage)
+
+        def step(c, carry):
+            add_branch(c)
+            push(gout.at[c], gin.at[c], s_hop.at[c], r_g.at[c], device(x, y, below, t))
+            multiply(gout, c)
+            hand_out(c)
+            add_up(c)
+            return carry
+
+        lax.fori_loop(0, CHUNKS, step, 0)
+
+    pl.when(z >= 2)(values_stage)
+
+    @pl.when(z == 7)
+    def _():
+        def step(c, carry):
+            add_branch(c)
+            hand_out(c)
+            return carry
+
+        lax.fori_loop(0, CHUNKS, step, 0)
 
     wait_bytes(xd, r_xd)
     wait_bytes(val.at[pl.ds(0, 3)], r_val)
@@ -240,16 +305,28 @@
 
     owner = 2 * x + t
     place = 8 * x + 4 * t + y
-
-    def owner_parts(t2):
-        yield 0, dvb.at[t2], vwin.at[pl.ds(pl.multiple_of(128 + y * 256, 128), 256)], 0, (z, owner, t2), None
-        yield 1, dvb.at[t2, pl.ds(128, 128)], vwin.at[pl.ds(0, 128)], 1, (z, owner + 1, t2), y == 3
-        yield 2, dvb.at[t2, pl.ds(0, 128)], vwin.at[pl.ds(1152, 128)], 2, (z, owner - 1, t2), jnp.logical_and(
-            y == 0, owner >= 1
-        )
-        for k in range(8):
-            yield 3 + k, dob.at[t2, pl.ds(32 * k, 64)], owin.at[place], 3, (z, 8 + k, t2), None
-        yield 11, dob.at[t2, pl.ds(16, 16)], owin.at[place, pl.ds(48, 16)], 3, (z, 7, t2), None
+    half = lax.rem(after, 2)
+
+    def mid_parts():
+        for t2 in range(2):
+            for q in range(2):
+                dst = mid.at[lax.div(after, 2), t2]
+                yield t2, q, dob.at[t2, pl.ds(128 * q, 160)], dst, device(x, y, 4 * half + 2 + q, t)
+
+    def owner_parts():
+        for t2 in range(2):
+            main = vwin.at[pl.ds(pl.multiple_of(128 + y * 256, 128), 256)]
+            yield t2, 0, dvb.at[t2], main, (after, owner, t2), None
+            yield t2, 1, dvb.at[t2, pl.ds(128, 128)], vwin.at[pl.ds(0, 128)], (after, owner + 1, t2), y == 3
+            low = jnp.logical_and(y == 0, owner >= 1)
+            yield t2, 2, dvb.at[t2, pl.ds(0, 128)], vwin.at[pl.ds(1152, 128)], (after, owner - 1, t2), low
+            yield t2, 3, dob.at[t2, pl.ds(16, 16)], owin.at[place, pl.ds(48, 16)], (after, 7, t2), None
+
+    def fin_parts(j):
+        for t2 in range(2):
+            for y2 in range(4):
+                to = (2 * j + zh, zl * 4 + y2, t2)
+                yield t2 * 4 + y2, mid.at[j, t2, pl.ds(32 * y2, 64)], owin.at[place], to
 
     def guarded(cond, what):
         if cond is None:
@@ -257,9 +334,18 @@
         else:
             pl.when(cond)(what)
 
-    for t2 in range(2):
-        for k, src, dst, r, to, cond in owner_parts(t2):
-            guarded(cond, functools.partial(send, src, dst, s_own.at[t2, k], r_own.at[r], to))
+    for t2, q, src, dst, to in mid_parts():
+        send(src, dst, s_mid.at[t2, q], r_mid.at[lax.div(after, 2), t2], to)
+    for t2, k, src, dst, to, cond in owner_parts():
+        guarded(cond, functools.partial(send, src, dst, s_own.at[t2, k], r_own.at[k], to))
+
+    @pl.when(zl >= 2)
+    def _():
+        for j in reversed(range(4)):
+            for t2 in range(2):
+                wait_bytes(mid.at[j, t2], r_mid.at[j, t2])
+            for k, src, dst, to in fin_parts(j):
+                send(src, dst, s_fin.at[j, k], r_own.at[3], to)
 
     @pl.when(dp <= 7)
     def _():
@@ -283,18 +369,27 @@
 
     wait_bytes(out, r_out)
 
-    sent(vw, s_w1.at[0], w1_to)
-    sent(ow, s_w1.at[1], w1_to)
+    sent(vw, s_wa.at[0], wa_to)
+    sent(ow, s_wa.at[1], wa_to)
 
     @pl.when(top_sender)
     def _():
-        for k, src, c, to in top_parts():
+        for k, src, dst, c, to in top_parts():
             sent(src, s_top.at[k], to)
 
+    for which in (1, 0):
+
+        @pl.when(x == zl)
+        def _():
+            for k, src, dst, to in w1_parts(which):
+                sent(src, s_w1.at[k, which], to)
+
+        for k, src, dst, to in w2_parts(which):
+            sent(src, s_w2.at[k, which], to)
+    for k, src, to in x_moves():
+        sent(src, s_x.at[k], to)
     for k, src, to in x_parts():
-        sent(src, s_x.at[k], to)
-    for k, src, dst, r, to in w2_parts():
-        sent(src, s_w2.at[k], to)
+        sent(src, s_xa.at[k], to)
     for k, src, to in xd_parts():
         sent(src, s_xd.at[k], to)
     wait_bytes(rsv, s_rsv)
@@ -304,24 +399,27 @@
 
     def drain(c, carry):
         wait_bytes(rsb.at[c], s_rs.at[c])
-        wait_bytes(rsb.at[c], s_ag.at[c])
+        wait_bytes(vg.at[y, c], s_ag.at[c])
+        wait_bytes(gout.at[c], s_hop.at[c])
         for k, src, to in gd_parts(c):
             sent(src, s_gd.at[c, k], to)
-
-        @pl.when(z > 0)
-        def _():
-            wait_bytes(gout.at[c], s_hop.at[c])
-
-        for k, src, to in out_parts(c):
+        for k, src, dst, to in out_parts(c):
             sent(src, s_out.at[c, k], to)
         for k, y2 in y_peers():
             wait_bytes(vg.at[y, c], s_vg.at[c, k])
         return carry
 
     lax.fori_loop(0, CHUNKS, drain, 0)
-    for t2 in range(2):
-        for k, src, dst, r, to, cond in owner_parts(t2):
-            guarded(cond, functools.partial(sent, src, s_own.at[t2, k], to))
+    for t2, q, src, dst, to in mid_parts():
+        sent(src, s_mid.at[t2, q], to)
+    for t2, k, src, dst, to, cond in owner_parts():
+        guarded(cond, functools.partial(sent, src, s_own.at[t2, k], to))
+
+    @pl.when(zl >= 2)
+    def _():
+        for j in range(4):
+            for k, src, dst, to in fin_parts(j):
+                sent(src, s_fin.at[j, k], to)
 
 
 def relay(xin, top, vw, ow):
@@ -337,32 +435,39 @@
         in_specs=[hbm] * 4,
         out_specs=(hbm, hbm, hbm),
         scratch_shapes=[
-            pltpu.VMEM((CHUNKS, 64, 1024), BF16),
-            pltpu.VMEM((CHUNKS, 64, 1024), BF16),
-            pltpu.VMEM((4, 2, 64, 1024), BF16),
+            pltpu.VMEM((CHUNKS, ROWS, 1024), BF16),
+            pltpu.VMEM((CHUNKS, ROWS, 1024), BF16),
+            pltpu.VMEM((CHUNKS, ROWS, 1024), BF16),
+            pltpu.VMEM((4, 128, 1024), BF16),
+            pltpu.VMEM((4, 4, 32, 1024), BF16),
+            pltpu.VMEM((4, 512, 256), BF16),
+            pltpu.VMEM((4, 256, 512), BF16),
             pltpu.VMEM((512, 256), BF16),
             pltpu.VMEM((256, 512), BF16),
             pltpu.VMEM((1024, 512), BF16),
             pltpu.VMEM((512, 1024), BF16),
-            pltpu.VMEM((CHUNKS, 64, 512), BF16),
-            pltpu.VMEM((CHUNKS, 7, 16, 256), BF16),
-            pltpu.VMEM((4, CHUNKS, 64, 512), BF16),
-            pltpu.VMEM((4, CHUNKS, 64, 256), BF16),
+            pltpu.VMEM((CHUNKS, ROWS, 512), BF16),
+            pltpu.VMEM((CHUNKS, 7, PIECE, 256), BF16),
+            pltpu.VMEM((CHUNKS, PIECE, 256), BF16),
+            pltpu.VMEM((4, CHUNKS, ROWS, 512), BF16),
+            pltpu.VMEM((4, CHUNKS, ROWS, 256), BF16),
             pltpu.VMEM((512, 512), BF16),
             pltpu.VMEM((7, 128, 256), BF16),
             pltpu.VMEM((4, 512, 512), BF16),
-            pltpu.VMEM((4, 4, 2, 64, 256), BF16),
+            pltpu.VMEM((4, 4, 128, 256), BF16),
             pltpu.VMEM((256, 512), F32),
             pltpu.VMEM((512, 256), F32),
             pltpu.VMEM((2, 256, 256), BF16),
             pltpu.VMEM((2, 288, 256), BF16),
-            dma((8,)), dma((2,)), dma((8,)), dma((8,)),
-            dma((CHUNKS,)), dma((CHUNKS,)), dma((CHUNKS,)), dma((CHUNKS, 4)),
+            pltpu.VMEM((4, 2, 160, 256), BF16),
+            dma((8,)), dma((4,)), dma((2,)), dma((4, 2)), dma((4, 2)), dma((8,)),
+            dma((CHUNKS,)), dma((CHUNKS,)), dma((CHUNKS,)), dma((CHUNKS, ROWS // 16)),
             dma((CHUNKS, 4)), dma((CHUNKS, 3)), dma, dma,
-            dma((3,)), dma((4,)), dma((2, 12)),
-            dma, dma((2,)), dma((2,)), dma((CHUNKS,)),
-            dma((CHUNKS,)), dma((CHUNKS,)), dma, dma, dma, dma,
-            dma, dma, dma((4,)), dma,
+            dma((3,)), dma((4,)), dma((2, 4)), dma((2, 2)), dma((4, 8)),
+            dma((4,)), dma, dma((4, 2)), dma((2,)), dma((2,)),
+            dma((CHUNKS,)), dma((CHUNKS,)), dma((CHUNKS,)), dma((CHUNKS,)),
+            dma, dma, dma, dma, dma, dma,
+            dma((4,)), dma((4, 2)), dma,
         ],
         compiler_params=pltpu.CompilerParams(has_side_effects=True, vmem_limit_bytes=48 * 1024 * 1024),
     )(xin, top, vw, ow)

time: 408 us -> 280 us (0.69)
  Pallas kernels: 400 us -> 271 us
    pallas_call x1, Pallas kernels: 395 us -> 265 us  [relay(): pl.pallas_call(relay_kernel, out_shape=(jax.ShapeDtypeStruct((4, 16, 8192...]
where the time goes in v3:
time: 280 us; the launch traced here: 278 us
  Pallas kernels  271 us (97%)
  local copies, waits for them, and re-layouts  6.63 us (2%)
    pallas_call x1, Pallas kernels, relay(): pl.pallas_call(relay_kernel, out_shape=(jax.ShapeDtypeStruct((4, 16, 8192...  265 us
    unnamed x17, local copies, waits for them, and re-layouts  6.63 us

profile of v3, /device:TPU:97, one launch (start us, length us, event | category | flops | bytes accessed | tf_op | source)
XLA Modules:
  0.0 278.2 jit_solution(15750474358679663728)
XLA Ops:
  0.6 0.0 copy-start.3
  0.6 1.2 copy-done.3
  1.9 0.0 copy-start.4
  1.9 1.2 copy-done.4
  3.1 0.0 copy-start.5
  3.1 0.9 copy-done.5
  4.0 0.0 copy-start.6
  4.0 0.9 copy-done.6
  5.0 0.0 copy-start
  5.0 0.0 copy-start.1
  5.0 0.0 copy-start.7
  5.0 265.4 %shard_map.111 = (bf16[4,16,8192]{2,1,0:T(8,128)(2,1)S(1)}, bf16[1280,256]{1,0:T(8,128)(2,1)S(1)}, bf16[32,64,256]{2,1,0:T(8,128)(2,1)S(1)}) custom-call(bf16[4,16,8192]{2,1,0:T(8,128)(2,1)S(1)} %bitcast.14, bf16[4,16,8192]{2,1,0:T(8,128)(2,1)S(1)} %copy-done.4, bf16[512,256]{1,0:T(8,128)(2,1)S(1)} %bitcast.16, bf16[256,512]{1,0:T(8,128)(2,1)S(1)} %bitcast.17), custom_call_target="tpu_custom_call" | custom-call | tf_op jit(solution)/shard_map/pallas_call | solution.py:428
  270.4 0.0 copy-done
  270.4 0.0 copy-done.1
  270.4 0.0 copy-done.7
  270.4 0.0 copy-start.2
  270.4 1.3 copy-done.2
  271.7 5.6 %shard_map.112 = (f32[2560,128]{1,0:T(8,128)}, f32[2560,128]{1,0:T(8,128)}, f32[2560,128]{1,0:T(8,128)}) custom-call(s32[16]{0:T(128)S(1)} %bitcast.18, bf16[1280,256]{1,0:T(8,128)(2,1)S(1)} %get-tuple-element.11.vwin, bf16[32,64,256]{2,1,0:T(8,128)(2,1)S(1)} %get-tuple-element.12.owin, f32[2560,128]{1,0:T(8,128)S(1)} %bitcast.11, f32[2560,128]{1,0:T(8,128)S(1)} %bitcast.12, ...), custom_call_target="tpu_custom_call" | custom-call | tf_op jit(solution)/shard_map/pallas_call | solution.py:527
  277.3 1.0 copy.13
Async XLA Ops:
  0.6 1.2 copy-start.3
  1.9 1.2 copy-start.4
  3.1 0.9 copy-start.5
  4.0 0.9 copy-start.6
  5.0 265.4 %copy-start = (f32[1,1,327680]{2,1,0:T(1,128)S(1)}, f32[1,1,327680]{2,1,0:T(1,128)}, u32[]{:S(2)}) copy-start(f32[1,1,327680]{2,1,0:T(1,128)} %param.13) | copy-start | bytes 3932164
  5.0 265.4 %copy-start.1 = (f32[1,1,327680]{2,1,0:T(1,128)S(1)}, f32[1,1,327680]{2,1,0:T(1,128)}, u32[]{:S(2)}) copy-start(f32[1,1,327680]{2,1,0:T(1,128)} %param.14) | copy-start | bytes 3932164
  5.0 265.4 %copy-start.7 = (s32[1,1,16]{2,1,0:T(1,128)S(1)}, s32[1,1,16]{2,1,0:T(1,128)}, u32[]{:S(2)}) copy-start(s32[1,1,16]{2,1,0:T(1,128)} %param.12) | copy-start | bytes 196
  270.4 1.3 copy-start.2

commit v4 on v3

--- a/solution.py
+++ b/solution.py
@@ -22,7 +22,9 @@
 CHUNKS = 8
 ROWS = 512 // CHUNKS
 PIECE = ROWS // 4
-MOVE_AT = 2
+PACED = 2
+GO_AT = 7
+MOVE_AT = 7
 NT = (((1,), (1,)), ((), ()))
 NN = (((1,), (0,)), ((), ()))
 TN = (((0,), (0,)), ((), ()))
@@ -51,7 +53,7 @@
     accv, acco, dvb, dob, mid,
     s_xa, s_x, s_wa, s_w1, s_w2, s_top, s_rs, s_ag, s_hop, s_out, s_gd, s_vg, s_rsv, s_agv, s_val, s_xd,
     s_own, s_mid, s_fin,
-    r_xa, r_x, r_wa, r_w1, r_w2, r_top, r_g, r_rs, r_ag, r_gd, r_vg, r_rsv, r_agv, r_val, r_xd, r_own, r_mid, r_out,
+    r_xa, r_x, r_wa, r_w1, r_w2, r_top, r_g, r_rs, r_ag, r_gd, r_vg, r_rsv, r_agv, r_val, r_xd, r_own, r_mid, r_out, go,
 ):
     sec = lax.axis_index("section")
     dp = lax.axis_index("dp")
@@ -200,9 +202,15 @@
             dst = out.at[mb, :, aligned(x * 2048 + t * 1024, 1024)]
             yield a, gout.at[c, pl.ds(a * 16, 16), :], dst, (after, z2 * 4 + y, t2)
 
-    def hand_out(c):
+    def rows_out(c):
         for k, src, dst, to in out_parts(c):
             send(src, dst, s_out.at[c, k], r_out, to)
+
+    def hand_out(c):
+        rows_out(c)
+        hand_in(c)
+
+    def hand_in(c):
         for k, y2 in y_peers():
             push(vg.at[y, c], vg.at[y, c], s_vg.at[c, k], r_vg, device(x, y2, z, t))
         for k, src, to in gd_parts(c):
@@ -243,8 +251,8 @@
     def _():
         def begin(c):
             wait_bytes(gtop.at[c], r_top.at[c])
+            multiply(gtop, c)
             push(gtop.at[c], gin.at[c], s_hop.at[c], r_g.at[c], device(x, y, below, t))
-            multiply(gtop, c)
 
         def step(c, carry):
             pl.when(c + 1 < CHUNKS)(lambda: begin(c + 1))
@@ -264,10 +272,11 @@
 
         def step(c, carry):
             add_branch(c)
+            multiply(gout, c)
             push(gout.at[c], gin.at[c], s_hop.at[c], r_g.at[c], device(x, y, below, t))
-            multiply(gout, c)
-            hand_out(c)
             add_up(c)
+            pl.when(z < PACED)(functools.partial(rows_out, c))
+            hand_in(c)
             return carry
 
         lax.fori_loop(0, CHUNKS, step, 0)
@@ -279,6 +288,26 @@
         def step(c, carry):
             add_branch(c)
             hand_out(c)
+
+            @pl.when(c == GO_AT)
+            def _():
+                for k in range(1, 8):
+                    pl.semaphore_signal(
+                        go, inc=1, device_id=device(x, y, lax.rem(z + k, 8), t), device_id_type=MESH
+                    )
+
+            return carry
+
+        lax.fori_loop(0, CHUNKS, step, 0)
+
+    paced = jnp.logical_and(z >= PACED, z < 7)
+
+    @pl.when(paced)
+    def _():
+        def step(c, carry):
+            rows_out(c)
+            for k, src, dst, to in out_parts(c):
+                sent(src, s_out.at[c, k], to)
             return carry
 
         lax.fori_loop(0, CHUNKS, step, 0)
@@ -333,6 +362,10 @@
             what()
         else:
             pl.when(cond)(what)
+
+    @pl.when(z < 7)
+    def _():
+        pl.semaphore_wait(go, 1)
 
     for t2, q, src, dst, to in mid_parts():
         send(src, dst, s_mid.at[t2, q], r_mid.at[lax.div(after, 2), t2], to)
@@ -403,8 +436,12 @@
         wait_bytes(gout.at[c], s_hop.at[c])
         for k, src, to in gd_parts(c):
             sent(src, s_gd.at[c, k], to)
-        for k, src, dst, to in out_parts(c):
-            sent(src, s_out.at[c, k], to)
+
+        @pl.when(jnp.logical_not(paced))
+        def _():
+            for k, src, dst, to in out_parts(c):
+                sent(src, s_out.at[c, k], to)
+
         for k, y2 in y_peers():
             wait_bytes(vg.at[y, c], s_vg.at[c, k])
         return carry
@@ -467,9 +504,9 @@
             dma((4,)), dma, dma((4, 2)), dma((2,)), dma((2,)),
             dma((CHUNKS,)), dma((CHUNKS,)), dma((CHUNKS,)), dma((CHUNKS,)),
             dma, dma, dma, dma, dma, dma,
-            dma((4,)), dma((4, 2)), dma,
+            dma((4,)), dma((4, 2)), dma, pltpu.SemaphoreType.REGULAR,
         ],
-        compiler_params=pltpu.CompilerParams(has_side_effects=True, vmem_limit_bytes=48 * 1024 * 1024),
+        compiler_params=pltpu.CompilerParams(has_side_effects=True, vmem_limit_bytes=60 * 1024 * 1024),
     )(xin, top, vw, ow)
 
 

time: 280 us -> 261 us (0.932); the launches traced: 278 us -> 256 us
  Pallas kernels: 271 us -> 251 us
    pallas_call x1, Pallas kernels: 265 us -> 245 us  [relay(): pl.pallas_call(relay_kernel, out_shape=(jax.ShapeDtypeStruct((4, 16, 8192...]
    unnamed x17 -> x15, local copies, waits for them, and re-layouts: 6.63 us -> 4.61 us
where the time goes in v4:
time: 261 us; the launch traced here: 256 us
  Pallas kernels  251 us (96%)
  local copies, waits for them, and re-layouts  4.61 us (2%)
    pallas_call x1, Pallas kernels, relay(): pl.pallas_call(relay_kernel, out_shape=(jax.ShapeDtypeStruct((4, 16, 8192...  245 us
    pallas_call x1, Pallas kernels, adam(): pl.pallas_call(functools.partial(adam_kernel, steps), grid=(steps,), out_...  5.55 us

profile of v4, /device:TPU:97, one launch (start us, length us, event | category | flops | bytes accessed | tf_op | source)
XLA Modules:
  0.0 256.0 jit_solution(6397845711533797663)
XLA Ops:
  0.6 0.0 copy-start
  0.6 0.0 copy-start.1
  0.7 0.0 copy-start.5
  0.7 245.1 %shard_map.111 = (bf16[4,16,8192]{2,1,0:T(8,128)(2,1)}, bf16[1280,256]{1,0:T(8,128)(2,1)}, bf16[32,64,256]{2,1,0:T(8,128)(2,1)}) custom-call(bf16[4,16,8192]{2,1,0:T(8,128)(2,1)} %bitcast.15, bf16[4,16,8192]{2,1,0:T(8,128)(2,1)} %top.1, bf16[512,256]{1,0:T(8,128)(2,1)} %bitcast.17, bf16[256,512]{1,0:T(8,128)(2,1)} %bitcast.18), custom_call_target="tpu_custom_call" | custom-call | tf_op jit(solution)/shard_map/pallas_call | solution.py:465
  245.8 0.0 copy-done
  245.8 0.0 copy-done.1
  245.8 0.0 copy-done.5
  245.8 0.0 copy-start.2
  245.8 1.3 copy-done.2
  247.1 0.0 copy-start.3
  247.1 1.2 copy-done.3
  248.3 0.0 copy-start.4
  248.3 1.1 copy-done.4
  249.4 0.0 copy-start.6
  249.4 5.6 %shard_map.112 = (f32[2560,128]{1,0:T(8,128)}, f32[2560,128]{1,0:T(8,128)}, f32[2560,128]{1,0:T(8,128)}) custom-call(s32[16]{0:T(128)S(1)} %bitcast.14, bf16[1280,256]{1,0:T(8,128)(2,1)S(1)} %copy-done.4, bf16[32,64,256]{2,1,0:T(8,128)(2,1)S(1)} %copy-done.3, f32[2560,128]{1,0:T(8,128)S(1)} %bitcast.11, f32[2560,128]{1,0:T(8,128)S(1)} %bitcast.12, ...), custom_call_target="tpu_custom_call" | custom-call | tf_op jit(solution)/shard_map/pallas_call | solution.py:564
  255.0 0.0 copy-done.6
  255.0 1.0 copy.13
Async XLA Ops:
  0.6 245.1 %copy-start = (f32[1,1,327680]{2,1,0:T(1,128)S(1)}, f32[1,1,327680]{2,1,0:T(1,128)}, u32[]{:S(2)}) copy-start(f32[1,1,327680]{2,1,0:T(1,128)} %param.13) | copy-start | bytes 3932164
  0.6 245.1 %copy-start.1 = (f32[1,1,327680]{2,1,0:T(1,128)S(1)}, f32[1,1,327680]{2,1,0:T(1,128)}, u32[]{:S(2)}) copy-start(f32[1,1,327680]{2,1,0:T(1,128)} %param.14) | copy-start | bytes 3932164
  0.7 245.1 %copy-start.5 = (s32[1,1,16]{2,1,0:T(1,128)S(1)}, s32[1,1,16]{2,1,0:T(1,128)}, u32[]{:S(2)}) copy-start(s32[1,1,16]{2,1,0:T(1,128)} %param.12) | copy-start | bytes 196
  245.8 1.3 copy-start.2
  247.1 1.2 copy-start.3
  248.3 1.1 copy-start.4
  249.4 5.6 %copy-start.6 = (bf16[4,16,8192]{2,1,0:T(8,128)(2,1)S(1)}, bf16[4,16,8192]{2,1,0:T(8,128)(2,1)}, u32[]{:S(2)}) copy-start(bf16[4,16,8192]{2,1,0:T(8,128)(2,1)} %get-tuple-element.10) | copy-start | bytes 3145732

commit v5 on v4

--- a/solution.py
+++ b/solution.py
@@ -23,7 +23,7 @@
 ROWS = 512 // CHUNKS
 PIECE = ROWS // 4
 PACED = 2
-GO_AT = 7
+GO_AT = 6
 MOVE_AT = 7
 NT = (((1,), (1,)), ((), ()))
 NN = (((1,), (0,)), ((), ()))

time: 261 us -> 259 us (level)
  the two profiles are of different devices: /device:TPU:97 before, /device:TPU:91 now
where the time goes in v5:
time: 259 us
  Pallas kernels  253 us (98%)
  local copies, waits for them, and re-layouts  4.61 us (2%)
    pallas_call x1, Pallas kernels, relay(): pl.pallas_call(relay_kernel, out_shape=(jax.ShapeDtypeStruct((4, 16, 8192...  248 us
    pallas_call x1, Pallas kernels, adam(): pl.pallas_call(functools.partial(adam_kernel, steps), grid=(steps,), out_...  5.54 us

profile of v5, /device:TPU:91, one launch (start us, length us, event | category | flops | bytes accessed | tf_op | source)
XLA Modules:
  0.0 258.8 jit_solution(11820812450269932758)
XLA Ops:
  0.6 0.0 copy-start
  0.6 0.0 copy-start.1
  0.7 0.0 copy-start.5
  0.7 247.9 %shard_map.111 = (bf16[4,16,8192]{2,1,0:T(8,128)(2,1)}, bf16[1280,256]{1,0:T(8,128)(2,1)}, bf16[32,64,256]{2,1,0:T(8,128)(2,1)}) custom-call(bf16[4,16,8192]{2,1,0:T(8,128)(2,1)} %bitcast.15, bf16[4,16,8192]{2,1,0:T(8,128)(2,1)} %top.1, bf16[512,256]{1,0:T(8,128)(2,1)} %bitcast.17, bf16[256,512]{1,0:T(8,128)(2,1)} %bitcast.18), custom_call_target="tpu_custom_call" | custom-call | tf_op jit(solution)/shard_map/pallas_call | solution.py:465
  248.6 0.0 copy-done
  248.6 0.0 copy-done.1
  248.6 0.0 copy-done.5
  248.6 0.0 copy-start.2
  248.7 1.3 copy-done.2
  250.0 0.0 copy-start.3
  250.0 1.2 copy-done.3
  251.2 0.0 copy-start.4
  251.2 1.1 copy-done.4
  252.3 0.0 copy-start.6
  252.3 5.5 %shard_map.112 = (f32[2560,128]{1,0:T(8,128)}, f32[2560,128]{1,0:T(8,128)}, f32[2560,128]{1,0:T(8,128)}) custom-call(s32[16]{0:T(128)S(1)} %bitcast.14, bf16[1280,256]{1,0:T(8,128)(2,1)S(1)} %copy-done.4, bf16[32,64,256]{2,1,0:T(8,128)(2,1)S(1)} %copy-done.3, f32[2560,128]{1,0:T(8,128)S(1)} %bitcast.11, f32[2560,128]{1,0:T(8,128)S(1)} %bitcast.12, ...), custom_call_target="tpu_custom_call" | custom-call | tf_op jit(solution)/shard_map/pallas_call | solution.py:564
  257.8 0.0 copy-done.6
  257.8 1.0 copy.13
Async XLA Ops:
  0.6 248.0 %copy-start = (f32[1,1,327680]{2,1,0:T(1,128)S(1)}, f32[1,1,327680]{2,1,0:T(1,128)}, u32[]{:S(2)}) copy-start(f32[1,1,327680]{2,1,0:T(1,128)} %param.13) | copy-start | bytes 3932164
  0.6 248.0 %copy-start.1 = (f32[1,1,327680]{2,1,0:T(1,128)S(1)}, f32[1,1,327680]{2,1,0:T(1,128)}, u32[]{:S(2)}) copy-start(f32[1,1,327680]{2,1,0:T(1,128)} %param.14) | copy-start | bytes 3932164
  0.7 248.0 %copy-start.5 = (s32[1,1,16]{2,1,0:T(1,128)S(1)}, s32[1,1,16]{2,1,0:T(1,128)}, u32[]{:S(2)}) copy-start(s32[1,1,16]{2,1,0:T(1,128)} %param.12) | copy-start | bytes 196
  248.6 1.3 copy-start.2
  250.0 1.2 copy-start.3
  251.2 1.1 copy-start.4
  252.3 5.5 %copy-start.6 = (bf16[4,16,8192]{2,1,0:T(8,128)(2,1)S(1)}, bf16[4,16,8192]{2,1,0:T(8,128)(2,1)}, u32[]{:S(2)}) copy-start(bf16[4,16,8192]{2,1,0:T(8,128)(2,1)} %get-tuple-element.10) | copy-start | bytes 3145732
